TPU v7x, 256 devices: a whole 4x4x8 slice. The times are simulated.
256 devices in a mesh: row: 32 (over y_lo, z, core), col: 8 (over y_hi, x).
Axes of the slice: x: 4, y: 4 (y_hi: 2, y_lo: 2; y = y_hi * 2 + y_lo), z: 8, core: 2. Of those that a mesh axis runs over, the one named last changes fastest.
Arguments:
- pair: float32 [512, 512, 128], P('row', 'col'), may hold values from -6 to 6
- pair_mask: int32 [512, 512], P('row', 'col'), may hold values 0 or 1
- in_gain: float32 [128], replicated, may hold values from 0.25 to 1.75
- in_bias: float32 [128], replicated, may hold values from -3 to 3
- w_in: bfloat16 [128, 640], replicated, may hold values from -0.5 to 0.5
- out_gain: float32 [128], replicated, may hold values from 0.25 to 1.75
- out_bias: float32 [128], replicated, may hold values from -3 to 3
- w_out: bfloat16 [128, 128], replicated, may hold values from -0.5 to 0.5
- cotangent: float32 [512, 512, 128], P('row', 'col'), may hold values from -6 to 6
Outputs:
- d_pair: float32 [512, 512, 128], P('row', 'col')
- d_w_in: float32 [128, 640], replicated
- d_w_out: float32 [128, 128], replicated
All inputs are finite; a program needn't handle non-finite values. No bound on the sum of `pair_mask` on one device may be relied on, other than what follows from the above.
Results may differ from a plain program's by a relative error of at most 0.014.
Values may be sent and summed in bfloat16 or wider, within the bound.
A program may use at most 128 MiB of HBM per device.

v0:
```python
import jax
import jax.numpy as jnp
from jax import lax
from jax.sharding import PartitionSpec as P


def layer_norm(values, gain, bias):
    centered = values - jnp.mean(values, axis=-1, keepdims=True)
    inverse = 1.0 / jnp.sqrt(jnp.mean(centered * centered, axis=-1, keepdims=True) + 1e-05)
    normed = centered * inverse
    return (normed * gain + bias, normed, inverse)


def norm_back(normed, inverse, d_normed):
    first = jnp.mean(d_normed, axis=-1, keepdims=True)
    second = jnp.mean(d_normed * normed, axis=-1, keepdims=True)
    return inverse * (d_normed - first - normed * second)


def body(pair, pair_mask, in_gain, in_bias, w_in, out_gain, out_bias, w_out, cotangent):
    tile_rows, tile_cols, width = pair.shape
    hidden = w_out.shape[0]
    zn_full, in_normed, in_inverse = layer_norm(pair, in_gain, in_bias)
    zn_flat = zn_full.astype(jnp.bfloat16).reshape(-1, width)
    proj = jnp.dot(zn_flat, w_in, preferred_element_type=jnp.float32).reshape(
        tile_rows, tile_cols, -1
    )
    value_a = proj[:, :, 0:hidden]
    gate_a = jax.nn.sigmoid(proj[:, :, hidden : 2 * hidden])
    value_b = proj[:, :, 2 * hidden : 3 * hidden]
    gate_b = jax.nn.sigmoid(proj[:, :, 3 * hidden : 4 * hidden])
    gate_out = jax.nn.sigmoid(proj[:, :, 4 * hidden :])
    mask_val = pair_mask.astype(jnp.float32)[:, :, None]
    left = (mask_val * gate_a * value_a).astype(jnp.bfloat16)
    right = (mask_val * gate_b * value_b).astype(jnp.bfloat16)
    right_panel = lax.all_gather(right, "row", axis=0, tiled=True)
    partial_value = jnp.einsum(
        "ikh,jkh->ijh", left, right_panel, preferred_element_type=jnp.float32
    )
    product = lax.psum_scatter(partial_value, "col", scatter_dimension=1, tiled=True)
    xn_full, mid_normed, mid_inverse = layer_norm(product, out_gain, out_bias)
    xn_flat = xn_full.astype(jnp.bfloat16).reshape(-1, hidden)
    mixed = jnp.dot(xn_flat, w_out, preferred_element_type=jnp.float32).reshape(
        tile_rows, tile_cols, width
    )
    d_go = cotangent * mixed * gate_out * (1.0 - gate_out)
    d_mixed = (cotangent * gate_out).astype(jnp.bfloat16).reshape(-1, width)
    d_w_out_part = jnp.dot(xn_flat.T, d_mixed, preferred_element_type=jnp.float32)
    d_xn = jnp.dot(d_mixed, w_out.T, preferred_element_type=jnp.float32).reshape(
        tile_rows, tile_cols, hidden
    )
    d_product = norm_back(mid_normed, mid_inverse, d_xn * out_gain).astype(jnp.bfloat16)
    dx_rows = lax.all_gather(d_product, "col", axis=1, tiled=True)
    d_left = jnp.einsum("ijh,jkh->ikh", dx_rows, right_panel, preferred_element_type=jnp.float32)
    d_right = lax.psum_scatter(
        jnp.einsum("ijh,ikh->jkh", dx_rows, left, preferred_element_type=jnp.float32).astype(
            jnp.bfloat16
        ),
        "row",
        scatter_dimension=0,
        tiled=True,
    ).astype(jnp.float32)
    d_pa = d_left * mask_val * gate_a
    d_ga = d_left * mask_val * value_a * gate_a * (1.0 - gate_a)
    d_pb = d_right * mask_val * gate_b
    d_gb = d_right * mask_val * value_b * gate_b * (1.0 - gate_b)
    d_proj = (
        jnp.concatenate([d_pa, d_ga, d_pb, d_gb, d_go], axis=-1)
        .astype(jnp.bfloat16)
        .reshape(-1, 4 * hidden + width)
    )
    d_w_in_part = jnp.dot(zn_flat.T, d_proj, preferred_element_type=jnp.float32)
    d_zn = jnp.dot(d_proj, w_in.T, preferred_element_type=jnp.float32).reshape(
        tile_rows, tile_cols, width
    )
    d_pair = norm_back(in_normed, in_inverse, d_zn * in_gain)
    d_w_in, d_w_out = lax.psum((d_w_in_part, d_w_out_part), ("row", "col"))
    return (d_pair, d_w_in, d_w_out)


def solution(mesh):
    placed = (
        P("row", "col", None),
        P("row", "col"),
        P(),
        P(),
        P(),
        P(),
        P(),
        P(),
        P("row", "col", None),
    )
    return jax.shard_map(
        body,
        mesh=mesh,
        in_specs=placed,
        out_specs=(P("row", "col", None), P(), P()),
        check_vma=False,
    )
```

profile of v0, /device:TPU:1, one launch (start us, length us, event | category | flops | bytes accessed | tf_op | source)
XLA Modules:
  0.0 703.2 jit_solution(17391979660597807167)
XLA Ops:
  8.0 1.3 reduce_sum.72
  9.3 1.4 multiply_reduce_fusion.3
  10.7 1.7 fusion.19
  12.4 1.2 multiply_convert_fusion.6
  13.7 1.4 copy.52
  15.1 75.2 %all-gather.3.cloned.1.call-done = bf16[512,64,128]{2,1,0:T(8,128)(2,1)} async-done(((bf16[16,64,128]{2,1,0:T(8,128)(2,1)}), bf16[512,64,128]{2,1,0:T(8,128)(2,1)}) %all-gather.3.cloned.1.call-update) | async-done | bytes 8388624 | tf_op jit(solution)/shard_map/all_gather | solution.py:36
  90.3 23.7 %copy.57 = bf16[512,64,128]{1,0,2:T(8,128)(2,1)} copy(bf16[512,64,128]{2,1,0:T(8,128)(2,1)} %all-gather.3.cloned.1.call-done) | data formatting | bytes 16777216 | tf_op jit(solution)/shard_map/all_gather | solution.py:36
  114.0 9.4 %convolution_bitcast_fusion = f32[16,512,128]{1,0,2:T(8,128)} fusion(bf16[512,64,128]{1,0,2:T(8,128)(2,1)} %copy.57, bf16[16,64,128]{1,0,2:T(8,128)(2,1)S(1)} %copy.52), kind=kOutput, calls=%fused_computation.1 | convolution fusion | flops 134217728 | bytes 12845056 | tf_op jit(solution)/shard_map/ikh,jkh->ijh/dot_general | solution.py:37
  123.4 5.8 copy.53
  129.3 88.4 %reduce-scatter.3.cloned.1.call-done = f32[16,64,128]{2,0,1:T(8,128)} async-done(((f32[16,512,128]{2,0,1:T(8,128)}), f32[16,64,128]{2,0,1:T(8,128)}) %reduce-scatter.3.cloned.1.call-update) | async-done | bytes 524304 | tf_op jit(solution)/shard_map/reduce_scatter | solution.py:40
  217.7 1.3 reduce_sum.74
  219.1 1.4 multiply_reduce_fusion.2
  220.6 1.9 fusion.24
  224.0 58.9 %all-gather.5.cloned.1.call-done = bf16[16,512,128]{2,0,1:T(8,128)(2,1)} async-done(((bf16[16,64,128]{2,0,1:T(8,128)(2,1)}), bf16[16,512,128]{2,0,1:T(8,128)(2,1)}) %all-gather.5.cloned.1.call-update) | async-done | bytes 2097168 | tf_op jit(solution)/shard_map/all_gather | solution.py:53
  282.9 4.9 copy.58
  287.8 7.4 %fusion.25 = bf16[128,64,512]{2,1,0:T(8,128)(2,1)} fusion(bf16[16,64,128]{1,0,2:T(8,128)(2,1)} %copy-done.3, bf16[16,512,128]{1,0,2:T(8,128)(2,1)} %copy.58), kind=kOutput, calls=%fused_computation.62 | convolution fusion | flops 134217728 | bytes 10747904 | tf_op jit(solution)/shard_map/ijh,ikh->jkh/dot_general | solution.py:56
  295.2 13.6 %copy.62 = bf16[128,64,512]{0,1,2:T(8,128)(2,1)} copy(bf16[128,64,512]{2,1,0:T(8,128)(2,1)} %fusion.25) | data formatting | bytes 16777216 | tf_op jit(solution)/shard_map/ijh,ikh->jkh/dot_general | solution.py:56
  309.5 2.2 convolution_bitcast_fusion.2
  311.7 9.8 %fusion.26 = f32[128,64,16]{1,2,0:T(8,128)} fusion(bf16[16,512,128]{1,0,2:T(8,128)(2,1)} %copy.58, bf16[512,64,128]{1,0,2:T(8,128)(2,1)} %copy.57), kind=kOutput, calls=%fused_computation.63 | convolution fusion | flops 134217728 | bytes 11010048 | tf_op jit(solution)/shard_map/ijh,jkh->ikh/dot_general | solution.py:54
  321.4 1.6 copy.59
  323.1 0.9 fusion.14
  324.0 1.0 fusion.15
  325.0 109.1 %reduce-scatter.5.cloned.1.call-done = bf16[16,64,128]{2,1,0:T(8,128)(2,1)} async-done(((bf16[512,64,128]{2,1,0:T(8,128)(2,1)}), bf16[16,64,128]{2,1,0:T(8,128)(2,1)}) %reduce-scatter.5.cloned.1.call-update) | async-done | bytes 262160 | tf_op jit(solution)/shard_map/reduce_scatter | solution.py:55
  434.1 1.9 fusion.16
  436.1 2.0 fusion.17
  438.0 2.5 fusion.3
  440.5 2.8 convolution_bitcast_fusion.1
  443.3 2.0 fusion.23
  445.4 1.4 subtract_multiply_fusion
  446.8 246.7 %all-reduce.3.cloned.1.call-done = (f32[128,640]{1,0:T(8,128)}, f32[128,128]{1,0:T(8,128)}) async-done(((f32[128,640]{1,0:T(8,128)}, f32[128,128]{1,0:T(8,128)}), (f32[128,640]{1,0:T(8,128)}, f32[128,128]{1,0:T(8,128)})) %all-reduce.3.cloned.1.call-update) | async-done | bytes 393232 | tf_op jit(solution)/shard_map/psum | solution.py:77
  693.5 1.7 copy.82
  695.2 1.5 copy.83
  (41 shorter events, 3.2 us)
Async XLA Ops:
  7.2 3.6 copy-start
  7.2 83.1 %all-gather.3.cloned.1.call-start = ((), (), s32[]{:S(2)}) async-start(), calls=%async_computation.2 | async-start | bytes 8650752 | tf_op jit(solution)/shard_map/all_gather | solution.py:36
  8.0 4.5 copy-start.4
  13.6 204.1 %reduce-scatter.3.cloned.1.call-start = ((), (), s32[]{:S(2)}) async-start(), calls=%async_computation.3 | async-start | bytes 4718592 | tf_op jit(solution)/shard_map/reduce_scatter | solution.py:40
  15.1 99.0 %copy-start.3 = (bf16[16,64,128]{1,0,2:T(8,128)(2,1)}, bf16[16,64,128]{1,0,2:T(8,128)(2,1)S(1)}, u32[]{:S(2)}) copy-start(bf16[16,64,128]{1,0,2:T(8,128)(2,1)S(1)} %copy.52) | copy-start | bytes 786436
  129.3 91.3 %copy-start.5 = (bf16[128,128]{1,0:T(8,128)(2,1)S(1)}, bf16[128,128]{1,0:T(8,128)(2,1)}, u32[]{:S(2)}) copy-start(bf16[128,128]{1,0:T(8,128)(2,1)} %param.16) | copy-start | bytes 98308
  129.3 91.3 %copy-start.8 = (f32[128]{0:T(128)S(1)}, f32[128]{0:T(128)}, u32[]{:S(2)}) copy-start(f32[128]{0:T(128)} %param.14) | copy-start | bytes 1540
  129.3 153.6 %all-gather.5.cloned.1.call-start = ((), (), s32[]{:S(2)}) async-start(), calls=%async_computation.4 | async-start | bytes 2359296 | tf_op jit(solution)/shard_map/all_gather | solution.py:53
  217.7 4.8 copy-start.2
  224.0 210.2 %reduce-scatter.5.cloned.1.call-start = ((), (), s32[]{:S(2)}) async-start(), calls=%async_computation.5 | async-start | bytes 8650752 | tf_op jit(solution)/shard_map/reduce_scatter | solution.py:55
  308.8 0.7 copy-start.9
  308.8 384.6 %all-reduce.3.cloned.1.call-start = ((), (), s32[]{:S(2)}) async-start(), calls=%async_computation.6 | async-start | bytes 786432 | tf_op jit(solution)/shard_map/psum | solution.py:77
  438.0 2.5 copy-start.1
  438.0 2.5 copy-start.6
  438.0 2.5 copy-start.7
Sparse Core Ops, SparseCore 0:
  13.8 76.4 all-gather.2
  129.4 88.2 reduce-scatter.2
  224.1 58.7 all-gather.4
  309.0 125.1 reduce-scatter.4
  445.5 247.9 all-reduce.2
where the time goes:
time: 705 us; the launch traced here: 703 us
  waiting for transfers between devices  578 us (82%)
  local copies, waits for them, and re-layouts  55.6 us (8%)
  matrix products  39.6 us (6%)
  other arithmetic  15.3 us (2%)
  between operations  13.9 us (2%)
    psum x1, waiting for transfers between devices, body(): d_w_in, d_w_out = lax.psum((d_w_in_part, d_w_out_part), ('row', 'col'))  247 us
    reduce_scatter x1, waiting for transfers between devices, body(): lax.psum_scatter(jnp.einsum('ijh,ikh->jkh', dx_rows, left, preferred_elem...  109 us
    reduce_scatter x1, waiting for transfers between devices, body(): lax.psum_scatter(partial_value, 'col', scatter_dimension=1, tiled=True)  88.4 us
    all_gather x1, waiting for transfers between devices, body(): right_panel = lax.all_gather(right, 'row', axis=0, tiled=True)  75.2 us
    all_gather x1, waiting for transfers between devices, body(): dx_rows = lax.all_gather(d_product, 'col', axis=1, tiled=True)  58.9 us
    all_gather x1, local copies, waits for them, and re-layouts, body(): right_panel = lax.all_gather(right, 'row', axis=0, tiled=True)  23.7 us
  transfers between devices with their start and end apart: 5, of which 5 were waited for; matrix products, arithmetic and copies ran while one was open for 3% of the time, Pallas kernels for 0%

commit v1 on v0

v1 whole, which is shorter than its diff:
```python
import functools

import jax
import jax.numpy as jnp
from jax import lax
from jax.experimental import pallas as pl
from jax.experimental.pallas import tpu as pltpu
from jax.sharding import PartitionSpec as P

BF = jnp.bfloat16
F32 = jnp.float32
COLS = 8
CHIPS = 16
T = 8
L = 128
EPS = 1e-05


def nn(a, b):
    return lax.dot_general(a, b, (((1,), (0,)), ((), ())), preferred_element_type=F32)


def nt(a, b):
    return lax.dot_general(a, b, (((1,), (1,)), ((), ())), preferred_element_type=F32)


def lanes(t):
    return pl.ds(pl.multiple_of(t * L, L), L)


def spread(vec_ref):
    return jnp.broadcast_to(vec_ref[...], (L, L)).T


def norm(x):
    cen = x - jnp.mean(x, axis=0, keepdims=True)
    inv = lax.rsqrt(jnp.mean(cen * cen, axis=0, keepdims=True) + EPS)
    return cen * inv, inv


def norm_back(normed, inv, dn):
    first = jnp.mean(dn, axis=0, keepdims=True)
    second = jnp.mean(dn * normed, axis=0, keepdims=True)
    return inv * (dn - first - normed * second)


def low_half(shape):
    return lax.broadcasted_iota(jnp.int32, shape, len(shape) - 1) < L // 2


def to_plane(src, work, out):
    for m in range(COLS // 2):
        for half in range(2):
            for t in range(T):
                work[m, half, :, t, :] = src[2 * m + half, :, t * L : (t + 1) * L].astype(F32)
    low = low_half((16, T, L))
    for m in range(COLS // 2):
        a, b = work[m, 0], work[m, 1]
        top = jnp.where(low, a, pltpu.roll(b, L // 2, 2))
        bottom = jnp.where(low, pltpu.roll(a, L // 2, 2), b)
        out[:, :, m * L : (m + 1) * L] = jnp.concatenate([top, bottom], axis=1).astype(BF)


def from_plane(src, work, out):
    low = low_half((16, T, L))
    for m in range(COLS // 2):
        x = src[:, :, m * L : (m + 1) * L].astype(F32)
        top, bottom = x[:, 0:T], x[:, T : 2 * T]
        work[m, 0] = jnp.where(low, top, pltpu.roll(bottom, L // 2, 2))
        work[m, 1] = jnp.where(low, pltpu.roll(top, L // 2, 2), bottom)
    for m in range(COLS // 2):
        for half in range(2):
            for t in range(T):
                out[2 * m + half, :, t * L : (t + 1) * L] = work[m, half, :, t, :].astype(BF)


def kernel(
    pair_ref, mask_ref, in_gain_ref, in_bias_ref, w_in_ref, out_gain_ref, out_bias_ref, w_out_ref, cot_ref,
    dpair_ref, dwin_ref, dwout_ref,
    gains, w_in_t, w_out_t, mask_rows, in_normed, in_inv, zn,
    fa1, fa2, fb1, fb2, sgo, fgo, dmix, dxn, xn, dproj,
    out_col, in_col, out_row, in_row, plane_l, plane_r, plane_d, work,
    part, part_out, part_in,
    w_send, w_recv, w_sum, w_all, w_full, w_gather,
    col_s, col_r, row_s, row_r, core_s, core_r, wt_s, wt_r,
):
    r, c = lax.axis_index("row"), lax.axis_index("col")
    q = lax.rem(r, 2)
    chip = r // 2
    mate = r + 1 - 2 * q
    flat = c * 2 + q

    barrier = pltpu.get_barrier_semaphore()

    def hello(row, col):
        pl.semaphore_signal(barrier, inc=1, device_id=(row, col), device_id_type=pl.DeviceIdType.MESH)

    @pl.loop(1, COLS)
    def _(j):
        hello(r, lax.rem(c + j, COLS))
        hello(mate, lax.rem(c + j, COLS))

    @pl.loop(1, CHIPS)
    def _(j):
        hello(2 * lax.rem(chip + j, CHIPS) + q, c)

    hello(mate, c)

    def remote(src, dst, ssem, rsem, row, col):
        return pltpu.make_async_remote_copy(
            src_ref=src, dst_ref=dst, send_sem=ssem, recv_sem=rsem,
            device_id=(row, col), device_id_type=pl.DeviceIdType.MESH,
        )

    def col_copy(n, j):
        to = lax.rem(c + j, COLS)
        return remote(out_col.at[n, to], in_col.at[n, c], col_s.at[n, j], col_r.at[n, c], r, to)

    def col_send(n):
        @pl.loop(1, COLS)
        def _(j):
            col_copy(n, j).start()

        pltpu.make_async_copy(out_col.at[n, c], in_col.at[n, c], col_r.at[n, c]).start()

    def col_wait(n):
        @pl.loop(0, COLS)
        def _(k):
            pltpu.make_async_copy(in_col.at[n, k], in_col.at[n, k], col_r.at[n, k]).wait()

    def row_copy(n, j, src, dst):
        to = lax.rem(chip + j, CHIPS)
        return remote(src(to), dst(chip), row_s.at[n, j], row_r.at[n, chip], 2 * to + q, c)

    def row_send(n, src, dst):
        @pl.loop(1, CHIPS)
        def _(j):
            row_copy(n, j, src, dst).start()

        pltpu.make_async_copy(src(chip), dst(chip), row_r.at[n, chip]).start()

    def row_wait(n, dst):
        @pl.loop(0, CHIPS)
        def _(k):
            pltpu.make_async_copy(dst(k), dst(k), row_r.at[n, k]).wait()

    def row_out(n):
        return lambda k: out_row.at[n, k]

    def row_in(n):
        return lambda k: in_row.at[n, k]

    right_rows = lambda k: plane_r.at[k, q]
    left_rows = lambda k: plane_l.at[k]
    grad_rows = lambda k: plane_d.at[k]

    gains[0] = spread(in_gain_ref)
    gains[1] = spread(in_bias_ref)
    gains[2] = spread(out_gain_ref)
    gains[3] = spread(out_bias_ref)
    w_in_t[...] = w_in_ref[...].astype(F32).T.astype(BF)
    w_out_t[...] = w_out_ref[...].astype(F32).T.astype(BF)
    mask_f = mask_ref[...].astype(F32)
    mask_rows[...] = jnp.concatenate([mask_f[0:T], mask_f[T : 2 * T]], axis=1)

    def side(t, rows, f1, f2, n):
        both = nn(w_in_t[rows : rows + 2 * L, :], zn[:, lanes(t)])
        value, gate = both[0:L], jax.nn.sigmoid(both[L : 2 * L])
        first = mask_rows[pl.ds(t, 1), :] * gate
        used = first * value
        f1[t] = first
        f2[t] = used * (1.0 - gate)
        out_col[n, :, :, lanes(t)] = used.astype(BF).reshape(COLS, 16, L)

    @pl.loop(0, T)
    def _(t):
        x = jnp.concatenate([pair_ref[t], pair_ref[t + T]], axis=0).T
        normed, inv = norm(x)
        in_normed[t] = normed
        in_inv[pl.ds(t, 1), :] = inv
        zn[:, lanes(t)] = (normed * gains[0] + gains[1]).astype(BF)
        side(t, 2 * L, fb1, fb2, 0)

    pl.semaphore_wait(barrier, 2 * (COLS - 1) + CHIPS - 1 + 1)
    col_send(0)

    @pl.loop(0, T)
    def _(t):
        side(t, 0, fa1, fa2, 1)

    col_send(1)

    col_wait(0)
    to_plane(in_col.at[0], work, out_row.at[0])
    row_send(0, row_out(0), right_rows)
    col_wait(1)
    to_plane(in_col.at[1], work, out_row.at[1])
    row_send(1, row_out(1), left_rows)

    @pl.loop(0, T)
    def _(t):
        gate = jax.nn.sigmoid(nn(w_in_t[4 * L : 5 * L, :], zn[:, lanes(t)]))
        cot = jnp.concatenate([cot_ref[t], cot_ref[t + T]], axis=0).T
        gated = cot * gate
        fgo[t] = gated * (1.0 - gate)
        mix = gated.astype(BF)
        dmix[:, lanes(t)] = mix
        dxn[t] = nn(w_out_ref[...], mix) * gains[2]

    row_wait(0, right_rows)
    swap_r = remote(plane_r.at[:, q], plane_r.at[:, q], core_s.at[0], core_r.at[0], mate, c)
    swap_r.start()
    row_wait(1, left_rows)
    pltpu.make_async_copy(plane_r.at[:, 1 - q], plane_r.at[:, 1 - q], core_r.at[0]).wait()

    out_row[2] = nt(plane_l[...].reshape(256, 512), plane_r[...].reshape(512, 512)).astype(BF).reshape(CHIPS, 16, 512)
    row_send(2, row_out(2), row_in(0))
    row_wait(2, row_in(0))
    from_plane(in_row.at[0], work, out_col.at[2])
    col_send(2)
    col_wait(2)

    @pl.loop(0, T)
    def _(t):
        normed, inv = norm(in_col[2, :, :, lanes(t)].reshape(L, L).astype(F32))
        xn[:, lanes(t)] = (normed * gains[2] + gains[3]).astype(BF)
        out_col[3, :, :, lanes(t)] = norm_back(normed, inv, dxn[t]).astype(BF).reshape(COLS, 16, L)

    col_send(3)

    @pl.loop(0, T)
    def _(t):
        dproj[4 * L : 5 * L, lanes(t)] = (fgo[t] * nn(w_out_t[...], xn[:, lanes(t)])).astype(BF)

    dwout_ref[...] = nt(xn[...], dmix[...])

    col_wait(3)
    to_plane(in_col.at[3], work, out_row.at[3])
    row_send(3, row_out(3), grad_rows)
    row_wait(3, grad_rows)

    grad = plane_d[...].reshape(256, 512)
    part[...] = nn(grad.astype(F32).T.astype(BF), plane_l[...].reshape(256, 512)).reshape(CHIPS, 2, 16, 512)
    part_out[...] = part[:, 1 - q].astype(BF)
    swap_d = remote(part_out, part_in, core_s.at[1], core_r.at[1], mate, c)
    swap_d.start()
    out_row[4] = nn(grad, plane_r[...].reshape(512, 512)).astype(BF).reshape(CHIPS, 16, 512)
    row_send(4, row_out(4), row_in(1))
    pltpu.make_async_copy(part_in, part_in, core_r.at[1]).wait()
    out_row[5] = (part[:, q] + part_in[...].astype(F32)).astype(BF)
    row_send(5, row_out(5), row_in(2))

    row_wait(4, row_in(1))
    from_plane(in_row.at[1], work, out_col.at[4])
    col_send(4)
    row_wait(5, row_in(2))
    from_plane(in_row.at[2], work, out_col.at[5])
    col_send(5)
    col_wait(4)

    @pl.loop(0, T)
    def _(t):
        d = in_col[4, :, :, lanes(t)].reshape(L, L).astype(F32)
        dproj[0:L, lanes(t)] = (d * fa1[t]).astype(BF)
        dproj[L : 2 * L, lanes(t)] = (d * fa2[t]).astype(BF)

    col_wait(5)

    @pl.loop(0, T)
    def _(t):
        d = in_col[5, :, :, lanes(t)].reshape(L, L).astype(F32)
        dproj[2 * L : 3 * L, lanes(t)] = (d * fb1[t]).astype(BF)
        dproj[3 * L : 4 * L, lanes(t)] = (d * fb2[t]).astype(BF)

    grads = jnp.concatenate([nt(zn[...], dproj[...]), dwout_ref[...]], axis=1).astype(BF)
    w_send[:, 0] = grads[:, 0 : 3 * L].reshape(COLS, 16, 3 * L)
    w_send[:, 1] = grads[:, 3 * L : 6 * L].reshape(COLS, 16, 3 * L)

    def near(j):
        to = lax.rem(flat + j, 2 * COLS)
        return to // 2, lax.rem(to, 2)

    def w1_copy(j):
        tc, tq = near(j)
        return remote(w_send.at[tc, tq], w_recv.at[flat], wt_s.at[0, j], wt_r.at[0, flat], 2 * chip + tq, tc)

    def w2_copy(j):
        to = lax.rem(chip + j, CHIPS)
        return remote(w_sum, w_all.at[chip], wt_s.at[1, j], wt_r.at[1, chip], 2 * to + q, c)

    def w3_copy(j):
        tc, tq = near(j)
        return remote(w_full, w_gather.at[c, q], wt_s.at[2, j], wt_r.at[2, flat], 2 * chip + tq, tc)

    def each(copy):
        @pl.loop(1, 16)
        def _(j):
            copy(j).start()

    each(w1_copy)
    pltpu.make_async_copy(w_send.at[c, q], w_recv.at[flat], wt_r.at[0, flat]).start()

    @pl.loop(0, T)
    def _(t):
        dn = nn(w_in_ref[...], dproj[:, lanes(t)]) * gains[0]
        d = norm_back(in_normed[t], in_inv[pl.ds(t, 1), :], dn).T
        dpair_ref[t] = d[0 : L // 2]
        dpair_ref[t + T] = d[L // 2 : L]

    @pl.loop(0, 16)
    def _(k):
        pltpu.make_async_copy(w_recv.at[k], w_recv.at[k], wt_r.at[0, k]).wait()

    w_sum[...] = jnp.sum(w_recv[...].astype(F32), axis=0).astype(BF)
    each(w2_copy)
    pltpu.make_async_copy(w_sum, w_all.at[chip], wt_r.at[1, chip]).start()

    @pl.loop(0, CHIPS)
    def _(k):
        pltpu.make_async_copy(w_all.at[k], w_all.at[k], wt_r.at[1, k]).wait()

    w_full[...] = jnp.sum(w_all[...].astype(F32), axis=0).astype(w_full.dtype)
    each(w3_copy)
    pltpu.make_async_copy(w_full, w_gather.at[c, q], wt_r.at[2, flat]).start()

    @pl.loop(0, COLS)
    def _(k):
        for core in range(2):
            pltpu.make_async_copy(w_gather.at[k, core], w_gather.at[k, core], wt_r.at[2, 2 * k + core]).wait()

    first = w_gather[:, 0].astype(F32).reshape(L, 3 * L)
    second = w_gather[:, 1].astype(F32).reshape(L, 3 * L)
    dwin_ref[:, 0 : 3 * L] = first
    dwin_ref[:, 3 * L : 5 * L] = second[:, 0 : 2 * L]
    dwout_ref[...] = second[:, 2 * L : 3 * L]

    for n in range(6):

        @pl.loop(1, COLS)
        def _(j):
            col_copy(n, j).wait_send()

    for n, dst in enumerate((right_rows, left_rows, row_in(0), grad_rows, row_in(1), row_in(2))):

        @pl.loop(1, CHIPS)
        def _(j):
            row_copy(n, j, row_out(n), dst).wait_send()

    swap_r.wait_send()
    swap_d.wait_send()

    @pl.loop(1, 16)
    def _(j):
        w1_copy(j).wait_send()
        w2_copy(j).wait_send()
        w3_copy(j).wait_send()


def body(pair, pair_mask, in_gain, in_bias, w_in, out_gain, out_bias, w_out, cotangent):
    V = pltpu.VMEM
    tile = lambda dtype: V((T, L, L), dtype)
    D = pltpu.SemaphoreType.DMA
    return pl.pallas_call(
        kernel,
        out_shape=(
            jax.ShapeDtypeStruct(pair.shape, F32),
            jax.ShapeDtypeStruct(w_in.shape, F32),
            jax.ShapeDtypeStruct(w_out.shape, F32),
        ),
        in_specs=[pl.BlockSpec(memory_space=pltpu.VMEM)] * 9,
        out_specs=[pl.BlockSpec(memory_space=pltpu.VMEM)] * 3,
        scratch_shapes=[
            V((4, L, L), F32), V((5 * L, L), BF), V((L, L), BF), V((T, L), F32), tile(F32), V((T, L), F32), V((L, T * L), BF),
            tile(F32), tile(F32), tile(F32), tile(F32), tile(F32), tile(F32), V((L, T * L), BF), tile(F32),
            V((L, T * L), BF), V((5 * L, T * L), BF),
            V((6, COLS, 16, T * L), BF), V((6, COLS, 16, T * L), BF),
            V((6, CHIPS, 16, 512), BF), V((3, CHIPS, 16, 512), BF),
            V((CHIPS, 16, 512), BF), V((CHIPS, 2, 16, 512), BF), V((CHIPS, 16, 512), BF), V((4, 2, 16, T, L), F32),
            V((CHIPS, 2, 16, 512), F32), V((CHIPS, 16, 512), BF), V((CHIPS, 16, 512), BF),
            V((COLS, 2, 16, 3 * L), BF), V((16, 16, 3 * L), BF), V((16, 3 * L), BF), V((CHIPS, 16, 3 * L), BF),
            V((16, 3 * L), F32), V((COLS, 2, 16, 3 * L), F32),
            D((6, COLS)), D((6, COLS)), D((6, CHIPS)), D((6, CHIPS)), D((2,)), D((2,)), D((3, 16)), D((3, 16)),
        ],
        compiler_params=pltpu.CompilerParams(
            collective_id=0, has_side_effects=True, vmem_limit_bytes=40 * 1024 * 1024
        ),
    )(
        pair, pair_mask, in_gain.reshape(1, L), in_bias.reshape(1, L), w_in,
        out_gain.reshape(1, L), out_bias.reshape(1, L), w_out, cotangent,
    )


def solution(mesh):
    placed = (
        P("row", "col", None),
        P("row", "col"),
        P(),
        P(),
        P(),
        P(),
        P(),
        P(),
        P("row", "col", None),
    )
    return jax.shard_map(
        body,
        mesh=mesh,
        in_specs=placed,
        out_specs=(P("row", "col", None), P(), P()),
        check_vma=False,
    )
```

time: 705 us -> 119 us (0.17)
  waiting for transfers between devices: 578 us -> 0 us
  Pallas kernels: 0 us -> 111 us
  local copies, waits for them, and re-layouts: 55.6 us -> 7.27 us
  matrix products: 39.6 us -> 0 us
  other arithmetic: 15.3 us -> 0 us
  between operations: 13.9 us -> 0.68 us
    psum x1 -> x0, waiting for transfers between devices: 247 us -> none  [body(): d_w_in, d_w_out = lax.psum((d_w_in_part, d_w_out_part), ('row', 'col'))]
    reduce_scatter x2 -> x0, waiting for transfers between devices: 197 us -> none  [the longest x1 109 us: body(): lax.psum_scatter(jnp.einsum('ijh,ikh->jkh', dx_rows, left, preferred_elem...]
    all_gather x2 -> x0, waiting for transfers between devices: 134 us -> none  [the longest x1 75.2 us: body(): right_panel = lax.all_gather(right, 'row', axis=0, tiled=True)]
    pallas_call x0 -> x1, Pallas kernels: none -> 111 us  [body(): pl.pallas_call(kernel, out_shape=(jax.ShapeDtypeStruct(pair.shape, F32),...]
    dot_general x9 -> x0, matrix products: 39.6 us -> none  [the longest x1 9.78 us: body(): jnp.einsum('ijh,jkh->ikh', dx_rows, right_panel, preferred_element_type=j...]
    all_gather x2 -> x0, local copies, waits for them, and re-layouts: 28.6 us -> none  [the longest x1 23.7 us: body(): right_panel = lax.all_gather(right, 'row', axis=0, tiled=True)]
    dot_general x2 -> x0, local copies, waits for them, and re-layouts: 15.2 us -> none  [the longest x1 13.6 us: body(): jnp.einsum('ijh,ikh->jkh', dx_rows, left, preferred_element_type=jnp.floa...]
  transfers between devices with their start and end apart: 5 -> 0, of which waited for: 5 -> 0; matrix products, arithmetic and copies ran while one was open for 3% -> 0% of each run, Pallas kernels for 0% -> 0%
where the time goes in v1:
time: 119 us
  Pallas kernels  111 us (93%)
  local copies, waits for them, and re-layouts  7.27 us (6%)
    pallas_call x1, Pallas kernels, body(): pl.pallas_call(kernel, out_shape=(jax.ShapeDtypeStruct(pair.shape, F32),...  111 us
    unnamed x21, local copies, waits for them, and re-layouts  7.27 us

profile of v1, /device:TPU:1, one launch (start us, length us, event | category | flops | bytes accessed | tf_op | source)
XLA Modules:
  0.0 118.8 jit_solution(2539101139685224942)
XLA Ops:
  0.6 0.0 copy-start.8
  0.6 0.0 copy-start.5
  0.7 0.0 copy-start.6
  0.7 0.0 copy-start.7
  0.7 0.6 copy-done.8
  1.3 0.0 copy-done.5
  1.3 0.0 copy-done.6
  1.3 0.0 copy-done.7
  1.3 0.0 copy-start
  1.3 1.0 copy-done
  2.4 0.0 copy-start.1
  2.4 1.0 copy-done.1
  3.4 0.0 copy-start.2
  3.4 0.9 copy-done.2
  4.3 0.0 copy-start.3
  4.3 0.8 copy-done.3
  5.1 0.0 copy-start.4
  5.1 0.7 copy-done.4
  5.8 110.8 %shard_map.112 = (f32[16,64,128]{2,1,0:T(8,128)S(1)}, f32[128,640]{1,0:T(8,128)S(1)}, f32[128,128]{1,0:T(8,128)S(1)}) custom-call(f32[16,64,128]{2,1,0:T(8,128)S(1)} %copy-done, s32[16,64]{1,0:T(8,128)S(1)} %copy-done.4, f32[1,128]{1,0:T(1,128)S(1)} %bitcast.4, f32[1,128]{1,0:T(1,128)S(1)} %bitcast.5, bf16[128,640]{1,0:T(8,128)(2,1)S(1)} %copy-done.2, ...), custom_call_target="tpu_custom_call" | custom-call | tf_op jit(solution)/shard_map/pallas_call | solution.py:363
  116.6 0.8 copy.15
  117.4 0.7 copy.16
  118.1 0.6 copy.17
Async XLA Ops:
  0.6 0.7 copy-start.8
  0.6 0.7 copy-start.5
  0.7 0.7 copy-start.6
  0.7 0.7 copy-start.7
  1.3 1.0 copy-start
  2.4 1.0 copy-start.1
  3.4 0.9 copy-start.2
  4.3 0.8 copy-start.3
  5.1 0.7 copy-start.4

commit v2 on v0

v2 whole, which is shorter than its diff:
```python
import functools

import jax
import jax.numpy as jnp
from jax import lax
from jax.experimental import pallas as pl
from jax.experimental.pallas import tpu as pltpu
from jax.sharding import PartitionSpec as P

BF = jnp.bfloat16
F32 = jnp.float32
COLS = 8
CHIPS = 16
DEPTH = 8
FAR_FIRST = (4, 3, 5, 2, 6, 1, 7, 0)
T = 8
L = 128
EPS = 1e-05


def nn(a, b):
    return lax.dot_general(a, b, (((1,), (0,)), ((), ())), preferred_element_type=F32)


def nt(a, b):
    return lax.dot_general(a, b, (((1,), (1,)), ((), ())), preferred_element_type=F32)


def spread(vec_ref):
    return jnp.broadcast_to(vec_ref[...], (L, L)).T


def norm(x):
    cen = x - jnp.mean(x, axis=0, keepdims=True)
    inv = lax.rsqrt(jnp.mean(cen * cen, axis=0, keepdims=True) + EPS)
    return cen * inv, inv


def norm_back(normed, inv, dn):
    first = jnp.mean(dn, axis=0, keepdims=True)
    second = jnp.mean(dn * normed, axis=0, keepdims=True)
    return inv * (dn - first - normed * second)


def low_half(shape):
    return lax.broadcasted_iota(jnp.int32, shape, len(shape) - 1) < L // 2


def join(src, m):
    low = low_half((CHIPS, T, L))
    a, b = src[:, 2 * m].astype(F32), src[:, 2 * m + 1].astype(F32)
    top = jnp.where(low, a, pltpu.roll(b, L // 2, 2))
    bottom = jnp.where(low, pltpu.roll(a, L // 2, 2), b)
    return jnp.concatenate([top, bottom], axis=1).astype(BF)


def split(x, out, m):
    low = low_half((CHIPS, T, L))
    x = x.reshape(CHIPS, 2 * T, L)
    top, bottom = x[:, 0:T], x[:, T : 2 * T]
    out[:, 2 * m] = jnp.where(low, top, pltpu.roll(bottom, L // 2, 2)).astype(BF)
    out[:, 2 * m + 1] = jnp.where(low, pltpu.roll(top, L // 2, 2), bottom).astype(BF)


def kernel(
    pair_ref, mask_ref, in_gain_ref, in_bias_ref, w_in_ref, out_gain_ref, out_bias_ref, w_out_ref, cot_ref,
    dpair_ref, dwin_ref, dwout_ref,
    gains, w_in_t, w_out_t, mask_rows, in_normed, in_inv, zn,
    fa1, fa2, fb1, fb2, fgo, dmix, dxn, xn, dproj, dwout,
    out_h, in_h, out_p, in_p, plane_l, plane_r, plane_d, grad_t, work_r, work_l,
    part_out, part_in,
    w_send, w_recv, w_sum, w_all, w_full, w_gather,
    leg_s, leg_r, core_s, core_r, wt_s, wt_r,
):
    r, c = lax.axis_index("row"), lax.axis_index("col")
    q = lax.rem(r, 2)
    chip = r // 2
    y, z = chip // DEPTH, lax.rem(chip, DEPTH)
    mate = r + 1 - 2 * q
    me = chip * COLS + c
    flat = (c * 2 + y) * 2 + q

    def every_chip(act):
        for dz in FAR_FIRST:

            @pl.loop(0 if dz else 1, 16)
            def _(k):
                to_y = lax.rem(y + k // COLS, 2)
                to_c = lax.rem(c + lax.rem(k, COLS), COLS)
                act(to_y * DEPTH + lax.rem(z + dz, DEPTH), to_c)

    barrier = pltpu.get_barrier_semaphore()

    def hello(row, col):
        pl.semaphore_signal(barrier, inc=1, device_id=(row, col), device_id_type=pl.DeviceIdType.MESH)

    every_chip(lambda to, col: hello(2 * to + q, col))

    @pl.loop(0, 16)
    def _(k):
        to_y = lax.rem(y + k // COLS, 2)
        hello(2 * (to_y * DEPTH + z) + 1 - q, lax.rem(c + lax.rem(k, COLS), COLS))

    def remote(src, dst, ssem, rsem, row, col):
        return pltpu.make_async_remote_copy(
            src_ref=src, dst_ref=dst, send_sem=ssem, recv_sem=rsem,
            device_id=(row, col), device_id_type=pl.DeviceIdType.MESH,
        )

    sent = []

    def leg_send(n, src, dst):
        every_chip(
            lambda to, col: remote(
                src.at[to * COLS + col], dst.at[me], leg_s.at[n], leg_r.at[n], 2 * to + q, col
            ).start()
        )
        pltpu.make_async_copy(src.at[me], dst.at[me], leg_r.at[n]).start()
        rest = src.at[0 : CHIPS * COLS - 1]
        sent.append(pltpu.make_async_copy(rest, rest, leg_s.at[n]).wait)

    def leg_wait(n, dst):
        pltpu.make_async_copy(dst, dst, leg_r.at[n]).wait()

    def blocks(ref):
        return ref[...].reshape(CHIPS, COLS, T, L)

    gains[0] = spread(in_gain_ref)
    gains[1] = spread(in_bias_ref)
    gains[2] = spread(out_gain_ref)
    gains[3] = spread(out_bias_ref)
    w_in_t[...] = w_in_ref[...].astype(F32).T.astype(BF)
    w_out_t[...] = w_out_ref[...].astype(F32).T.astype(BF)
    mask_f = mask_ref[...].astype(F32)
    mask_rows[...] = jnp.concatenate([mask_f[0:T], mask_f[T : 2 * T]], axis=1)

    def side(t, rows, f1, f2, work):
        both = nn(w_in_t[rows : rows + 2 * L, :], zn[:, t * L : (t + 1) * L])
        value, gate = both[0:L], jax.nn.sigmoid(both[L : 2 * L])
        first = mask_rows[t : t + 1, :] * gate
        used = first * value
        f1[t] = first
        f2[t] = used * (1.0 - gate)
        work[:, t, :] = used

    for t in range(T):
        x = jnp.concatenate([pair_ref[t], pair_ref[t + T]], axis=0).T
        normed, inv = norm(x)
        in_normed[t] = normed
        in_inv[t : t + 1, :] = inv
        zn[:, t * L : (t + 1) * L] = (normed * gains[0] + gains[1]).astype(BF)
        side(t, 2 * L, fb1, fb2, work_r)
    out_h[0] = work_r[...].astype(BF)

    pl.semaphore_wait(barrier, CHIPS * COLS - 1 + 16)
    leg_send(0, out_h.at[0], in_p.at[0])

    for t in range(T):
        side(t, 0, fa1, fa2, work_l)
    out_h[1] = work_l[...].astype(BF)
    leg_send(1, out_h.at[1], in_p.at[1])

    for t in range(T):
        gate = jax.nn.sigmoid(nn(w_in_t[4 * L : 5 * L, :], zn[:, t * L : (t + 1) * L]))
        cot = jnp.concatenate([cot_ref[t], cot_ref[t + T]], axis=0).T
        gated = cot * gate
        fgo[t] = gated * (1.0 - gate)
        mix = gated.astype(BF)
        dmix[:, t * L : (t + 1) * L] = mix
        dxn[:, t, :] = nn(w_out_ref[...], mix) * gains[2]

    leg_wait(0, in_p.at[0])
    for m in range(COLS // 2):
        plane_r[:, q, :, m * L : (m + 1) * L] = join(blocks(in_p.at[0]), m)
    swap_r = remote(plane_r.at[:, q], plane_r.at[:, q], core_s.at[0], core_r.at[0], mate, c)
    swap_r.start()
    sent.append(swap_r.wait_send)
    leg_wait(1, in_p.at[1])
    for m in range(COLS // 2):
        plane_l[:, :, m * L : (m + 1) * L] = join(blocks(in_p.at[1]), m)
    pltpu.make_async_copy(plane_r.at[:, 1 - q], plane_r.at[:, 1 - q], core_r.at[0]).wait()

    for m in range(COLS // 2):
        rows = plane_r[4 * m : 4 * m + 4].reshape(L, 512)
        split(nt(plane_l[...].reshape(256, 512), rows), out_p.at[0], m)
    leg_send(2, out_p.at[0].reshape(CHIPS * COLS, T, L), in_h.at[0])
    leg_wait(2, in_h.at[0])

    normed, inv = norm(in_h[0].astype(F32))
    work_r[...] = normed
    out_h[2] = norm_back(normed, inv, dxn[...]).astype(BF)
    leg_send(3, out_h.at[2], in_p.at[2])

    for t in range(T):
        some = (work_r[:, t, :] * gains[2] + gains[3]).astype(BF)
        xn[:, t * L : (t + 1) * L] = some
        dproj[4 * L : 5 * L, t * L : (t + 1) * L] = (fgo[t] * nn(w_out_t[...], some)).astype(BF)
    dwout[...] = nt(xn[...], dmix[...])

    leg_wait(3, in_p.at[2])
    for m in range(COLS // 2):
        some = join(blocks(in_p.at[2]), m)
        plane_d[:, :, m * L : (m + 1) * L] = some
        grad_t[4 * m : 4 * m + 4] = some.reshape(256, L).astype(F32).T.astype(BF).reshape(4, 2, 16, 256)

    part_out[...] = nn(grad_t[:, 1 - q].reshape(256, 256), plane_l[...].reshape(256, 512)).astype(BF)
    swap_d = remote(part_out, part_in, core_s.at[1], core_r.at[1], mate, c)
    swap_d.start()
    sent.append(swap_d.wait_send)
    for m in range(COLS // 2):
        cols = plane_r[:, :, :, m * L : (m + 1) * L].reshape(512, L)
        split(nn(plane_d[...].reshape(256, 512), cols), out_p.at[1], m)
    leg_send(4, out_p.at[1].reshape(CHIPS * COLS, T, L), in_h.at[1])
    pltpu.make_async_copy(part_in, part_in, core_r.at[1]).wait()
    for m in range(COLS // 2):
        cols = plane_l[:, :, m * L : (m + 1) * L].reshape(256, L)
        own = nn(grad_t[:, q].reshape(256, 256), cols)
        split(own + part_in[:, m * L : (m + 1) * L].astype(F32), out_p.at[2], m)
    leg_send(5, out_p.at[2].reshape(CHIPS * COLS, T, L), in_h.at[2])

    leg_wait(4, in_h.at[1])
    work_l[...] = in_h[1].astype(F32)
    for t in range(T):
        d = work_l[:, t, :]
        dproj[0:L, t * L : (t + 1) * L] = (d * fa1[t]).astype(BF)
        dproj[L : 2 * L, t * L : (t + 1) * L] = (d * fa2[t]).astype(BF)
    leg_wait(5, in_h.at[2])
    work_r[...] = in_h[2].astype(F32)
    for t in range(T):
        d = work_r[:, t, :]
        dproj[2 * L : 3 * L, t * L : (t + 1) * L] = (d * fb1[t]).astype(BF)
        dproj[3 * L : 4 * L, t * L : (t + 1) * L] = (d * fb2[t]).astype(BF)

    grads = jnp.concatenate([nt(zn[...], dproj[...]), dwout[...]], axis=1).astype(BF)
    w_send[:, 0] = grads[:, 0 : 3 * L].reshape(16, 8, 3 * L)
    w_send[:, 1] = grads[:, 3 * L : 6 * L].reshape(16, 8, 3 * L)

    def near(j):
        to = lax.rem(flat + j, 32)
        return to // 2, lax.rem(to, 2), 2 * (lax.rem(to // 2, 2) * DEPTH + z) + lax.rem(to, 2), to // 4

    def w1_copy(j):
        block, core, row, col = near(j)
        return remote(w_send.at[block, core], w_recv.at[flat], wt_s.at[0], wt_r.at[0], row, col)

    def w2_copy(j):
        row = 2 * (y * DEPTH + lax.rem(z + j, DEPTH)) + q
        return remote(w_sum, w_all.at[z], wt_s.at[1], wt_r.at[1], row, c)

    def w3_copy(j):
        block, core, row, col = near(j)
        return remote(w_full, w_gather.at[flat], wt_s.at[2], wt_r.at[2], row, col)

    def each(copy, count, n, whole):
        @pl.loop(1, count)
        def _(j):
            copy(j).start()

        rest = whole.at[0 : count - 1]
        sent.append(pltpu.make_async_copy(rest, rest, wt_s.at[n]).wait)

    each(w1_copy, 32, 0, w_recv)
    pltpu.make_async_copy(w_send.at[c * 2 + y, q], w_recv.at[flat], wt_r.at[0]).start()

    for t in range(T):
        dn = nn(w_in_ref[...], dproj[:, t * L : (t + 1) * L]) * gains[0]
        d = norm_back(in_normed[t], in_inv[t : t + 1, :], dn).T
        dpair_ref[t] = d[0 : L // 2]
        dpair_ref[t + T] = d[L // 2 : L]

    pltpu.make_async_copy(w_recv, w_recv, wt_r.at[0]).wait()
    w_sum[...] = jnp.sum(w_recv[...].astype(F32), axis=0).astype(BF)
    each(w2_copy, DEPTH, 1, w_all)
    pltpu.make_async_copy(w_sum, w_all.at[z], wt_r.at[1]).start()
    pltpu.make_async_copy(w_all, w_all, wt_r.at[1]).wait()
    w_full[...] = jnp.sum(w_all[...].astype(F32), axis=0).astype(BF)
    each(w3_copy, 32, 2, w_gather)
    pltpu.make_async_copy(w_full, w_gather.at[flat], wt_r.at[2]).start()
    pltpu.make_async_copy(w_gather, w_gather, wt_r.at[2]).wait()

    whole = w_gather[...].astype(F32).reshape(16, 2, 8, 3 * L)
    first, second = whole[:, 0].reshape(L, 3 * L), whole[:, 1].reshape(L, 3 * L)
    dwin_ref[:, 0 : 3 * L] = first
    dwin_ref[:, 3 * L : 5 * L] = second[:, 0 : 2 * L]
    dwout_ref[...] = second[:, 2 * L : 3 * L]

    for wait in sent:
        wait()


def body(pair, pair_mask, in_gain, in_bias, w_in, out_gain, out_bias, w_out, cotangent):
    V = pltpu.VMEM
    tile = lambda dtype: V((T, L, L), dtype)
    D = pltpu.SemaphoreType.DMA
    return pl.pallas_call(
        kernel,
        out_shape=(
            jax.ShapeDtypeStruct(pair.shape, F32),
            jax.ShapeDtypeStruct(w_in.shape, F32),
            jax.ShapeDtypeStruct(w_out.shape, F32),
        ),
        in_specs=[pl.BlockSpec(memory_space=pltpu.VMEM)] * 9,
        out_specs=[pl.BlockSpec(memory_space=pltpu.VMEM)] * 3,
        scratch_shapes=[
            V((4, L, L), F32), V((5 * L, L), BF), V((L, L), BF), V((T, L), F32), tile(F32), V((T, L), F32), V((L, T * L), BF),
            tile(F32), tile(F32), tile(F32), tile(F32), tile(F32), V((L, T * L), BF), V((L, T, L), F32),
            V((L, T * L), BF), V((5 * L, T * L), BF), V((L, L), F32),
            V((3, L, T, L), BF), V((3, L, T, L), BF),
            V((3, CHIPS, COLS, T, L), BF), V((3, L, T, L), BF),
            V((CHIPS, 16, 512), BF), V((CHIPS, 2, 16, 512), BF), V((CHIPS, 16, 512), BF), V((CHIPS, 2, 16, 256), BF),
            V((L, T, L), F32), V((L, T, L), F32),
            V((256, 512), BF), V((256, 512), BF),
            V((16, 2, 8, 3 * L), BF), V((32, 8, 3 * L), BF), V((8, 3 * L), BF), V((DEPTH, 8, 3 * L), BF),
            V((8, 3 * L), BF), V((32, 8, 3 * L), BF),
            D((6,)), D((6,)), D((2,)), D((2,)), D((3,)), D((3,)),
        ],
        compiler_params=pltpu.CompilerParams(
            collective_id=0, has_side_effects=True, vmem_limit_bytes=60 * 1024 * 1024
        ),
    )(
        pair, pair_mask, in_gain.reshape(1, L), in_bias.reshape(1, L), w_in,
        out_gain.reshape(1, L), out_bias.reshape(1, L), w_out, cotangent,
    )


def solution(mesh):
    placed = (
        P("row", "col", None),
        P("row", "col"),
        P(),
        P(),
        P(),
        P(),
        P(),
        P(),
        P("row", "col", None),
    )
    return jax.shard_map(
        body,
        mesh=mesh,
        in_specs=placed,
        out_specs=(P("row", "col", None), P(), P()),
        check_vma=False,
    )
```

time: 705 us -> 90 us (0.13)
  waiting for transfers between devices: 578 us -> 0 us
  Pallas kernels: 0 us -> 85.8 us
  local copies, waits for them, and re-layouts: 55.6 us -> 3.43 us
  matrix products: 39.6 us -> 0 us
  other arithmetic: 15.3 us -> 0 us
  between operations: 13.9 us -> 0.65 us
    psum x1 -> x0, waiting for transfers between devices: 247 us -> none  [body(): d_w_in, d_w_out = lax.psum((d_w_in_part, d_w_out_part), ('row', 'col'))]
    reduce_scatter x2 -> x0, waiting for transfers between devices: 197 us -> none  [the longest x1 109 us: body(): lax.psum_scatter(jnp.einsum('ijh,ikh->jkh', dx_rows, left, preferred_elem...]
    all_gather x2 -> x0, waiting for transfers between devices: 134 us -> none  [the longest x1 75.2 us: body(): right_panel = lax.all_gather(right, 'row', axis=0, tiled=True)]
    pallas_call x0 -> x1, Pallas kernels: none -> 85.8 us  [body(): pl.pallas_call(kernel, out_shape=(jax.ShapeDtypeStruct(pair.shape, F32),...]
    dot_general x9 -> x0, matrix products: 39.6 us -> none  [the longest x1 9.78 us: body(): jnp.einsum('ijh,jkh->ikh', dx_rows, right_panel, preferred_element_type=j...]
    all_gather x2 -> x0, local copies, waits for them, and re-layouts: 28.6 us -> none  [the longest x1 23.7 us: body(): right_panel = lax.all_gather(right, 'row', axis=0, tiled=True)]
    dot_general x2 -> x0, local copies, waits for them, and re-layouts: 15.2 us -> none  [the longest x1 13.6 us: body(): jnp.einsum('ijh,ikh->jkh', dx_rows, left, preferred_element_type=jnp.floa...]
  transfers between devices with their start and end apart: 5 -> 0, of which waited for: 5 -> 0; matrix products, arithmetic and copies ran while one was open for 3% -> 0% of each run, Pallas kernels for 0% -> 0%
where the time goes in v2:
time: 90 us; the launch traced here: 89.8 us
  Pallas kernels  85.8 us (95%)
  local copies, waits for them, and re-layouts  3.43 us (4%)
    pallas_call x1, Pallas kernels, body(): pl.pallas_call(kernel, out_shape=(jax.ShapeDtypeStruct(pair.shape, F32),...  85.8 us
    unnamed x7, local copies, waits for them, and re-layouts  3.43 us

profile of v2, /device:TPU:1, one launch (start us, length us, event | category | flops | bytes accessed | tf_op | source)
XLA Modules:
  0.0 89.8 jit_solution(392835587348078245)
XLA Ops:
  0.6 85.8 %shard_map.112 = (f32[16,64,128]{2,1,0:T(8,128)}, f32[128,640]{1,0:T(8,128)}, f32[128,128]{1,0:T(8,128)}) custom-call(f32[16,64,128]{2,1,0:T(8,128)} %pair_ref.1, s32[16,64]{1,0:T(8,128)} %mask_ref.1, f32[1,128]{1,0:T(1,128)} %bitcast.4, f32[1,128]{1,0:T(1,128)} %bitcast.5, bf16[128,640]{1,0:T(8,128)(2,1)} %w_in_ref.1, f32[1,128]{1,0:T(1,128)} %bitcast.6, ...), custom_call_target="tpu_custom_call" | custom-call | tf_op jit(solution)/shard_map/pallas_call | solution.py:295
  86.4 0.0 copy-start
  86.4 1.9 %copy.15 = f32[16,64,128]{2,1,0:T(8,128)} copy(f32[16,64,128]{2,1,0:T(8,128)} %get-tuple-element.6) | data formatting | bytes 1048576
  88.3 0.0 copy-done
  88.3 0.0 copy-start.1
  88.3 0.7 copy.16
  89.1 0.1 copy-done.1
  89.2 0.6 copy.17
Async XLA Ops:
  86.4 1.9 %copy-start = (f32[128,640]{1,0:T(8,128)S(1)}, f32[128,640]{1,0:T(8,128)}, u32[]{:S(2)}) copy-start(f32[128,640]{1,0:T(8,128)} %get-tuple-element.7) | copy-start | bytes 983044
  88.3 0.9 copy-start.1

commit v3 on v2

--- a/solution.py
+++ b/solution.py
@@ -13,6 +13,7 @@
 CHIPS = 16
 DEPTH = 8
 FAR_FIRST = (4, 3, 5, 2, 6, 1, 7, 0)
+UNROLL = 3
 T = 8
 L = 128
 EPS = 1e-05
@@ -63,11 +64,12 @@
 
 
 def kernel(
-    pair_ref, mask_ref, in_gain_ref, in_bias_ref, w_in_ref, out_gain_ref, out_bias_ref, w_out_ref, cot_ref,
-    dpair_ref, dwin_ref, dwout_ref,
+    pair_hbm, mask_ref, in_gain_ref, in_bias_ref, w_in_hbm, out_gain_ref, out_bias_ref, w_out_hbm, cot_hbm,
+    dpair_hbm, gather_ref,
+    pair_ref, w_in_ref, w_out_ref, cot_ref, dpair_ref, io_sem,
     gains, w_in_t, w_out_t, mask_rows, in_normed, in_inv, zn,
     fa1, fa2, fb1, fb2, fgo, dmix, dxn, xn, dproj, dwout,
-    out_h, in_h, out_p, in_p, plane_l, plane_r, plane_d, grad_t, work_r, work_l,
+    out_h2, in_p2, out_p, in_h, out_h, in_p, out_p2, in_h2, plane_l, plane_r, plane_d, grad_t, work_r, work_l,
     part_out, part_in,
     w_send, w_recv, w_sum, w_all, w_full, w_gather,
     leg_s, leg_r, core_s, core_r, wt_s, wt_r,
@@ -80,14 +82,28 @@
     me = chip * COLS + c
     flat = (c * 2 + y) * 2 + q
 
+    loads = [
+        pltpu.make_async_copy(src, dst, io_sem.at[n])
+        for n, (src, dst) in enumerate(
+            ((pair_hbm, pair_ref), (w_in_hbm, w_in_ref), (w_out_hbm, w_out_ref), (cot_hbm, cot_ref))
+        )
+    ]
+    for load in loads:
+        load.start()
+
+    levels = [lax.rem(z + dz, DEPTH) for dz in FAR_FIRST]
+
     def every_chip(act):
-        for dz in FAR_FIRST:
-
-            @pl.loop(0 if dz else 1, 16)
-            def _(k):
-                to_y = lax.rem(y + k // COLS, 2)
-                to_c = lax.rem(c + lax.rem(k, COLS), COLS)
-                act(to_y * DEPTH + lax.rem(z + dz, DEPTH), to_c)
+        for level in levels[:-1]:
+            act(y * DEPTH + level, c)
+
+        @pl.loop(1, 16, unroll=UNROLL)
+        def _(k):
+            k = 16 - k
+            base = lax.rem(y + k // COLS, 2) * DEPTH
+            col = lax.rem(c + lax.rem(k, COLS), COLS)
+            for level in levels:
+                act(base + level, col)
 
     barrier = pltpu.get_barrier_semaphore()
 
@@ -122,13 +138,15 @@
     def leg_wait(n, dst):
         pltpu.make_async_copy(dst, dst, leg_r.at[n]).wait()
 
-    def blocks(ref):
-        return ref[...].reshape(CHIPS, COLS, T, L)
+    def pair_blocks(side):
+        return in_p2[:, side].reshape(CHIPS, COLS, T, L)
 
     gains[0] = spread(in_gain_ref)
     gains[1] = spread(in_bias_ref)
     gains[2] = spread(out_gain_ref)
     gains[3] = spread(out_bias_ref)
+    for load in loads[:3]:
+        load.wait()
     w_in_t[...] = w_in_ref[...].astype(F32).T.astype(BF)
     w_out_t[...] = w_out_ref[...].astype(F32).T.astype(BF)
     mask_f = mask_ref[...].astype(F32)
@@ -150,16 +168,16 @@
         in_inv[t : t + 1, :] = inv
         zn[:, t * L : (t + 1) * L] = (normed * gains[0] + gains[1]).astype(BF)
         side(t, 2 * L, fb1, fb2, work_r)
-    out_h[0] = work_r[...].astype(BF)
+    out_h2[:, 0] = work_r[...].astype(BF)
+
+    for t in range(T):
+        side(t, 0, fa1, fa2, work_l)
+    out_h2[:, 1] = work_l[...].astype(BF)
 
     pl.semaphore_wait(barrier, CHIPS * COLS - 1 + 16)
-    leg_send(0, out_h.at[0], in_p.at[0])
-
-    for t in range(T):
-        side(t, 0, fa1, fa2, work_l)
-    out_h[1] = work_l[...].astype(BF)
-    leg_send(1, out_h.at[1], in_p.at[1])
-
+    leg_send(0, out_h2, in_p2)
+
+    loads[3].wait()
     for t in range(T):
         gate = jax.nn.sigmoid(nn(w_in_t[4 * L : 5 * L, :], zn[:, t * L : (t + 1) * L]))
         cot = jnp.concatenate([cot_ref[t], cot_ref[t + T]], axis=0).T
@@ -169,27 +187,26 @@
         dmix[:, t * L : (t + 1) * L] = mix
         dxn[:, t, :] = nn(w_out_ref[...], mix) * gains[2]
 
-    leg_wait(0, in_p.at[0])
-    for m in range(COLS // 2):
-        plane_r[:, q, :, m * L : (m + 1) * L] = join(blocks(in_p.at[0]), m)
+    leg_wait(0, in_p2)
+    for m in range(COLS // 2):
+        plane_r[:, q, :, m * L : (m + 1) * L] = join(pair_blocks(0), m)
     swap_r = remote(plane_r.at[:, q], plane_r.at[:, q], core_s.at[0], core_r.at[0], mate, c)
     swap_r.start()
     sent.append(swap_r.wait_send)
-    leg_wait(1, in_p.at[1])
-    for m in range(COLS // 2):
-        plane_l[:, :, m * L : (m + 1) * L] = join(blocks(in_p.at[1]), m)
+    for m in range(COLS // 2):
+        plane_l[:, :, m * L : (m + 1) * L] = join(pair_blocks(1), m)
     pltpu.make_async_copy(plane_r.at[:, 1 - q], plane_r.at[:, 1 - q], core_r.at[0]).wait()
 
     for m in range(COLS // 2):
         rows = plane_r[4 * m : 4 * m + 4].reshape(L, 512)
-        split(nt(plane_l[...].reshape(256, 512), rows), out_p.at[0], m)
-    leg_send(2, out_p.at[0].reshape(CHIPS * COLS, T, L), in_h.at[0])
-    leg_wait(2, in_h.at[0])
-
-    normed, inv = norm(in_h[0].astype(F32))
+        split(nt(plane_l[...].reshape(256, 512), rows), out_p, m)
+    leg_send(1, out_p.reshape(CHIPS * COLS, T, L), in_h)
+    leg_wait(1, in_h)
+
+    normed, inv = norm(in_h[...].astype(F32))
     work_r[...] = normed
-    out_h[2] = norm_back(normed, inv, dxn[...]).astype(BF)
-    leg_send(3, out_h.at[2], in_p.at[2])
+    out_h[...] = norm_back(normed, inv, dxn[...]).astype(BF)
+    leg_send(2, out_h, in_p)
 
     for t in range(T):
         some = (work_r[:, t, :] * gains[2] + gains[3]).astype(BF)
@@ -197,9 +214,9 @@
         dproj[4 * L : 5 * L, t * L : (t + 1) * L] = (fgo[t] * nn(w_out_t[...], some)).astype(BF)
     dwout[...] = nt(xn[...], dmix[...])
 
-    leg_wait(3, in_p.at[2])
-    for m in range(COLS // 2):
-        some = join(blocks(in_p.at[2]), m)
+    leg_wait(2, in_p)
+    for m in range(COLS // 2):
+        some = join(in_p[...].reshape(CHIPS, COLS, T, L), m)
         plane_d[:, :, m * L : (m + 1) * L] = some
         grad_t[4 * m : 4 * m + 4] = some.reshape(256, L).astype(F32).T.astype(BF).reshape(4, 2, 16, 256)
 
@@ -209,23 +226,21 @@
     sent.append(swap_d.wait_send)
     for m in range(COLS // 2):
         cols = plane_r[:, :, :, m * L : (m + 1) * L].reshape(512, L)
-        split(nn(plane_d[...].reshape(256, 512), cols), out_p.at[1], m)
-    leg_send(4, out_p.at[1].reshape(CHIPS * COLS, T, L), in_h.at[1])
+        split(nn(plane_d[...].reshape(256, 512), cols), out_p2.at[:, :, 0], m)
     pltpu.make_async_copy(part_in, part_in, core_r.at[1]).wait()
     for m in range(COLS // 2):
         cols = plane_l[:, :, m * L : (m + 1) * L].reshape(256, L)
         own = nn(grad_t[:, q].reshape(256, 256), cols)
-        split(own + part_in[:, m * L : (m + 1) * L].astype(F32), out_p.at[2], m)
-    leg_send(5, out_p.at[2].reshape(CHIPS * COLS, T, L), in_h.at[2])
-
-    leg_wait(4, in_h.at[1])
-    work_l[...] = in_h[1].astype(F32)
+        split(own + part_in[:, m * L : (m + 1) * L].astype(F32), out_p2.at[:, :, 1], m)
+    leg_send(3, out_p2.reshape(CHIPS * COLS, 2, T, L), in_h2)
+
+    leg_wait(3, in_h2)
+    work_l[...] = in_h2[:, 0].astype(F32)
+    work_r[...] = in_h2[:, 1].astype(F32)
     for t in range(T):
         d = work_l[:, t, :]
         dproj[0:L, t * L : (t + 1) * L] = (d * fa1[t]).astype(BF)
         dproj[L : 2 * L, t * L : (t + 1) * L] = (d * fa2[t]).astype(BF)
-    leg_wait(5, in_h.at[2])
-    work_r[...] = in_h[2].astype(F32)
     for t in range(T):
         d = work_r[:, t, :]
         dproj[2 * L : 3 * L, t * L : (t + 1) * L] = (d * fb1[t]).astype(BF)
@@ -268,6 +283,8 @@
         dpair_ref[t] = d[0 : L // 2]
         dpair_ref[t + T] = d[L // 2 : L]
 
+    store = pltpu.make_async_copy(dpair_ref, dpair_hbm, io_sem.at[4])
+    store.start()
     pltpu.make_async_copy(w_recv, w_recv, wt_r.at[0]).wait()
     w_sum[...] = jnp.sum(w_recv[...].astype(F32), axis=0).astype(BF)
     each(w2_copy, DEPTH, 1, w_all)
@@ -278,41 +295,47 @@
     pltpu.make_async_copy(w_full, w_gather.at[flat], wt_r.at[2]).start()
     pltpu.make_async_copy(w_gather, w_gather, wt_r.at[2]).wait()
 
-    whole = w_gather[...].astype(F32).reshape(16, 2, 8, 3 * L)
+    gather_ref[...] = w_gather[...]
+    store.wait()
+
+    for wait in sent:
+        wait()
+
+
+def finish_kernel(dpair_in, gather_ref, dpair_out, dwin_ref, dwout_ref, sem):
+    move = pltpu.make_async_copy(dpair_in, dpair_out, sem)
+    move.start()
+    whole = gather_ref[...].astype(F32).reshape(16, 2, 8, 3 * L)
     first, second = whole[:, 0].reshape(L, 3 * L), whole[:, 1].reshape(L, 3 * L)
     dwin_ref[:, 0 : 3 * L] = first
     dwin_ref[:, 3 * L : 5 * L] = second[:, 0 : 2 * L]
     dwout_ref[...] = second[:, 2 * L : 3 * L]
-
-    for wait in sent:
-        wait()
+    move.wait()
 
 
 def body(pair, pair_mask, in_gain, in_bias, w_in, out_gain, out_bias, w_out, cotangent):
     V = pltpu.VMEM
     tile = lambda dtype: V((T, L, L), dtype)
     D = pltpu.SemaphoreType.DMA
-    return pl.pallas_call(
+    vmem, hbm = pl.BlockSpec(memory_space=pltpu.VMEM), pl.BlockSpec(memory_space=pl.ANY)
+    d_pair, gathered = pl.pallas_call(
         kernel,
-        out_shape=(
-            jax.ShapeDtypeStruct(pair.shape, F32),
-            jax.ShapeDtypeStruct(w_in.shape, F32),
-            jax.ShapeDtypeStruct(w_out.shape, F32),
-        ),
-        in_specs=[pl.BlockSpec(memory_space=pltpu.VMEM)] * 9,
-        out_specs=[pl.BlockSpec(memory_space=pltpu.VMEM)] * 3,
+        out_shape=(jax.ShapeDtypeStruct(pair.shape, F32), jax.ShapeDtypeStruct((32, 8, 3 * L), BF)),
+        in_specs=[hbm, vmem, vmem, vmem, hbm, vmem, vmem, hbm, hbm],
+        out_specs=(hbm, vmem),
         scratch_shapes=[
+            V(pair.shape, F32), V(w_in.shape, BF), V(w_out.shape, BF), V(pair.shape, F32), V(pair.shape, F32), D((5,)),
             V((4, L, L), F32), V((5 * L, L), BF), V((L, L), BF), V((T, L), F32), tile(F32), V((T, L), F32), V((L, T * L), BF),
             tile(F32), tile(F32), tile(F32), tile(F32), tile(F32), V((L, T * L), BF), V((L, T, L), F32),
             V((L, T * L), BF), V((5 * L, T * L), BF), V((L, L), F32),
-            V((3, L, T, L), BF), V((3, L, T, L), BF),
-            V((3, CHIPS, COLS, T, L), BF), V((3, L, T, L), BF),
+            V((L, 2, T, L), BF), V((L, 2, T, L), BF), V((CHIPS, COLS, T, L), BF), V((L, T, L), BF),
+            V((L, T, L), BF), V((L, T, L), BF), V((CHIPS, COLS, 2, T, L), BF), V((L, 2, T, L), BF),
             V((CHIPS, 16, 512), BF), V((CHIPS, 2, 16, 512), BF), V((CHIPS, 16, 512), BF), V((CHIPS, 2, 16, 256), BF),
             V((L, T, L), F32), V((L, T, L), F32),
             V((256, 512), BF), V((256, 512), BF),
             V((16, 2, 8, 3 * L), BF), V((32, 8, 3 * L), BF), V((8, 3 * L), BF), V((DEPTH, 8, 3 * L), BF),
             V((8, 3 * L), BF), V((32, 8, 3 * L), BF),
-            D((6,)), D((6,)), D((2,)), D((2,)), D((3,)), D((3,)),
+            D((4,)), D((4,)), D((2,)), D((2,)), D((3,)), D((3,)),
         ],
         compiler_params=pltpu.CompilerParams(
             collective_id=0, has_side_effects=True, vmem_limit_bytes=60 * 1024 * 1024
@@ -321,6 +344,17 @@
         pair, pair_mask, in_gain.reshape(1, L), in_bias.reshape(1, L), w_in,
         out_gain.reshape(1, L), out_bias.reshape(1, L), w_out, cotangent,
     )
+    return pl.pallas_call(
+        finish_kernel,
+        out_shape=(
+            jax.ShapeDtypeStruct(pair.shape, F32),
+            jax.ShapeDtypeStruct(w_in.shape, F32),
+            jax.ShapeDtypeStruct(w_out.shape, F32),
+        ),
+        in_specs=[hbm, vmem],
+        out_specs=(hbm, vmem, vmem),
+        scratch_shapes=[D],
+    )(d_pair, gathered)
 
 
 def solution(mesh):

time: 90 us -> 109 us (1.21)
  Pallas kernels: 85.8 us -> 108 us
  local copies, waits for them, and re-layouts: 3.43 us -> 0 us
    pallas_call x0 -> x1, Pallas kernels: none -> 18.7 us  [body(): pl.pallas_call(finish_kernel, out_shape=(jax.ShapeDtypeStruct(pair.shape,...]
    unnamed x7 -> x0, local copies, waits for them, and re-layouts: 3.43 us -> none
    pallas_call x1, Pallas kernels: 85.8 us -> 89.2 us  [body(): pl.pallas_call(kernel, out_shape=(jax.ShapeDtypeStruct(pair.shape, F32),...]
where the time goes in v3:
time: 109 us; the launch traced here: 108 us
  Pallas kernels  108 us (99%)
    pallas_call x1, Pallas kernels, body(): pl.pallas_call(kernel, out_shape=(jax.ShapeDtypeStruct(pair.shape, F32),...  89.2 us
    pallas_call x1, Pallas kernels, body(): pl.pallas_call(finish_kernel, out_shape=(jax.ShapeDtypeStruct(pair.shape,...  18.7 us

profile of v3, /device:TPU:1, one launch (start us, length us, event | category | flops | bytes accessed | tf_op | source)
XLA Modules:
  0.0 108.5 jit_solution(4915381136494963688)
XLA Ops:
  0.6 89.2 %shard_map.112 = (f32[16,64,128]{2,1,0:T(8,128)}, bf16[32,8,384]{2,1,0:T(8,128)(2,1)}) custom-call(f32[16,64,128]{2,1,0:T(8,128)} %pair_hbm.1, s32[16,64]{1,0:T(8,128)} %mask_ref.1, f32[1,128]{1,0:T(1,128)} %bitcast.4, f32[1,128]{1,0:T(1,128)} %bitcast.5, bf16[128,640]{1,0:T(8,128)(2,1)} %w_in_hbm.1, f32[1,128]{1,0:T(1,128)} %bitcast.6, f32[1,128]{1,0:T(1,128)} %bitcast.7, ...), custom_call_target="tpu_custom_call" | custom-call | tf_op jit(solution)/shard_map/pallas_call | solution.py:321
  89.8 18.7 %shard_map.113 = (f32[16,64,128]{2,1,0:T(8,128)}, f32[128,640]{1,0:T(8,128)}, f32[128,128]{1,0:T(8,128)}) custom-call(f32[16,64,128]{2,1,0:T(8,128)} %get-tuple-element.5.dpair_in, bf16[32,8,384]{2,1,0:T(8,128)(2,1)} %get-tuple-element.6.gather_ref), custom_call_target="tpu_custom_call" | custom-call | tf_op jit(solution)/shard_map/pallas_call | solution.py:347

commit v4 on v2

--- a/solution.py
+++ b/solution.py
@@ -13,6 +13,7 @@
 CHIPS = 16
 DEPTH = 8
 FAR_FIRST = (4, 3, 5, 2, 6, 1, 7, 0)
+UNROLL = 3
 T = 8
 L = 128
 EPS = 1e-05
@@ -63,8 +64,9 @@
 
 
 def kernel(
-    pair_ref, mask_ref, in_gain_ref, in_bias_ref, w_in_ref, out_gain_ref, out_bias_ref, w_out_ref, cot_ref,
-    dpair_ref, dwin_ref, dwout_ref,
+    pair_hbm, mask_ref, in_gain_ref, in_bias_ref, w_in_hbm, out_gain_ref, out_bias_ref, w_out_hbm, cot_hbm,
+    dpair_hbm, gather_ref,
+    pair_ref, w_in_ref, w_out_ref, cot_ref, dpair_ref, io_sem, planes,
     gains, w_in_t, w_out_t, mask_rows, in_normed, in_inv, zn,
     fa1, fa2, fb1, fb2, fgo, dmix, dxn, xn, dproj, dwout,
     out_h, in_h, out_p, in_p, plane_l, plane_r, plane_d, grad_t, work_r, work_l,
@@ -80,26 +82,53 @@
     me = chip * COLS + c
     flat = (c * 2 + y) * 2 + q
 
+    loads = [
+        pltpu.make_async_copy(src, dst, io_sem.at[n])
+        for n, (src, dst) in enumerate(
+            ((pair_hbm, pair_ref), (w_in_hbm, w_in_ref), (w_out_hbm, w_out_ref), (cot_hbm, cot_ref))
+        )
+    ]
+    for load in loads:
+        load.start()
+
+    levels = [lax.rem(z + dz, DEPTH) for dz in FAR_FIRST]
+
+    def place(k):
+        return lax.rem(y + k // COLS, 2) * DEPTH, lax.rem(c + lax.rem(k, COLS), COLS)
+
+    def near_chips(act):
+        for level in levels[:-1]:
+            act(y * DEPTH + level, c)
+
+        @pl.loop(1, 16, unroll=UNROLL)
+        def _(k):
+            base, col = place(16 - k)
+            act(base + z, col)
+
+    def far_chips(act):
+        @pl.loop(1, 16, unroll=UNROLL)
+        def _(k):
+            base, col = place(16 - k)
+            for level in levels[:-1]:
+                act(base + level, col)
+
     def every_chip(act):
-        for dz in FAR_FIRST:
-
-            @pl.loop(0 if dz else 1, 16)
-            def _(k):
-                to_y = lax.rem(y + k // COLS, 2)
-                to_c = lax.rem(c + lax.rem(k, COLS), COLS)
-                act(to_y * DEPTH + lax.rem(z + dz, DEPTH), to_c)
+        for level in levels[:-1]:
+            act(y * DEPTH + level, c)
+
+        @pl.loop(1, 16, unroll=UNROLL)
+        def _(k):
+            base, col = place(16 - k)
+            for level in levels:
+                act(base + level, col)
 
     barrier = pltpu.get_barrier_semaphore()
 
-    def hello(row, col):
-        pl.semaphore_signal(barrier, inc=1, device_id=(row, col), device_id_type=pl.DeviceIdType.MESH)
-
-    every_chip(lambda to, col: hello(2 * to + q, col))
-
-    @pl.loop(0, 16)
-    def _(k):
-        to_y = lax.rem(y + k // COLS, 2)
-        hello(2 * (to_y * DEPTH + z) + 1 - q, lax.rem(c + lax.rem(k, COLS), COLS))
+    def hello(semaphore, row, col):
+        pl.semaphore_signal(semaphore, inc=1, device_id=(row, col), device_id_type=pl.DeviceIdType.MESH)
+
+    near_chips(lambda to, col: hello(barrier, 2 * to + q, col))
+    hello(barrier, mate, c)
 
     def remote(src, dst, ssem, rsem, row, col):
         return pltpu.make_async_remote_copy(
@@ -109,12 +138,13 @@
 
     sent = []
 
-    def leg_send(n, src, dst):
-        every_chip(
-            lambda to, col: remote(
-                src.at[to * COLS + col], dst.at[me], leg_s.at[n], leg_r.at[n], 2 * to + q, col
-            ).start()
-        )
+    def leg_send(n, src, dst, which=None):
+        def send(to, col):
+            remote(src.at[to * COLS + col], dst.at[me], leg_s.at[n], leg_r.at[n], 2 * to + q, col).start()
+
+        (which or every_chip)(send)
+        if which is near_chips:
+            return
         pltpu.make_async_copy(src.at[me], dst.at[me], leg_r.at[n]).start()
         rest = src.at[0 : CHIPS * COLS - 1]
         sent.append(pltpu.make_async_copy(rest, rest, leg_s.at[n]).wait)
@@ -129,6 +159,8 @@
     gains[1] = spread(in_bias_ref)
     gains[2] = spread(out_gain_ref)
     gains[3] = spread(out_bias_ref)
+    for load in loads[:3]:
+        load.wait()
     w_in_t[...] = w_in_ref[...].astype(F32).T.astype(BF)
     w_out_t[...] = w_out_ref[...].astype(F32).T.astype(BF)
     mask_f = mask_ref[...].astype(F32)
@@ -152,14 +184,20 @@
         side(t, 2 * L, fb1, fb2, work_r)
     out_h[0] = work_r[...].astype(BF)
 
-    pl.semaphore_wait(barrier, CHIPS * COLS - 1 + 16)
-    leg_send(0, out_h.at[0], in_p.at[0])
+    pl.semaphore_wait(barrier, DEPTH - 1 + 15 + 1)
+    for level in levels[:-1]:
+        hello(planes, 2 * (y * DEPTH + level) + q, c)
+    hello(planes, mate, c)
+    leg_send(0, out_h.at[0], in_p.at[0], near_chips)
+    pl.semaphore_wait(planes, DEPTH)
+    leg_send(0, out_h.at[0], in_p.at[0], far_chips)
 
     for t in range(T):
         side(t, 0, fa1, fa2, work_l)
     out_h[1] = work_l[...].astype(BF)
     leg_send(1, out_h.at[1], in_p.at[1])
 
+    loads[3].wait()
     for t in range(T):
         gate = jax.nn.sigmoid(nn(w_in_t[4 * L : 5 * L, :], zn[:, t * L : (t + 1) * L]))
         cot = jnp.concatenate([cot_ref[t], cot_ref[t + T]], axis=0).T
@@ -191,32 +229,32 @@
     out_h[2] = norm_back(normed, inv, dxn[...]).astype(BF)
     leg_send(3, out_h.at[2], in_p.at[2])
 
+    leg_wait(3, in_p.at[2])
+    for m in range(COLS // 2):
+        some = join(blocks(in_p.at[2]), m)
+        plane_d[:, :, m * L : (m + 1) * L] = some
+        grad_t[4 * m : 4 * m + 4] = some.reshape(256, L).astype(F32).T.astype(BF).reshape(4, 2, 16, 256)
+
+    part_out[...] = nn(grad_t[:, 1 - q].reshape(256, 256), plane_l[...].reshape(256, 512)).astype(BF)
+    swap_d = remote(part_out, part_in, core_s.at[1], core_r.at[1], mate, c)
+    swap_d.start()
+    sent.append(swap_d.wait_send)
+    for m in range(COLS // 2):
+        cols = plane_r[:, :, :, m * L : (m + 1) * L].reshape(512, L)
+        split(nn(plane_d[...].reshape(256, 512), cols), out_p.at[1], m)
+    leg_send(4, out_p.at[1].reshape(CHIPS * COLS, T, L), in_h.at[1])
+    pltpu.make_async_copy(part_in, part_in, core_r.at[1]).wait()
+    for m in range(COLS // 2):
+        cols = plane_l[:, :, m * L : (m + 1) * L].reshape(256, L)
+        own = nn(grad_t[:, q].reshape(256, 256), cols)
+        split(own + part_in[:, m * L : (m + 1) * L].astype(F32), out_p.at[2], m)
+    leg_send(5, out_p.at[2].reshape(CHIPS * COLS, T, L), in_h.at[2])
+
     for t in range(T):
         some = (work_r[:, t, :] * gains[2] + gains[3]).astype(BF)
         xn[:, t * L : (t + 1) * L] = some
         dproj[4 * L : 5 * L, t * L : (t + 1) * L] = (fgo[t] * nn(w_out_t[...], some)).astype(BF)
     dwout[...] = nt(xn[...], dmix[...])
-
-    leg_wait(3, in_p.at[2])
-    for m in range(COLS // 2):
-        some = join(blocks(in_p.at[2]), m)
-        plane_d[:, :, m * L : (m + 1) * L] = some
-        grad_t[4 * m : 4 * m + 4] = some.reshape(256, L).astype(F32).T.astype(BF).reshape(4, 2, 16, 256)
-
-    part_out[...] = nn(grad_t[:, 1 - q].reshape(256, 256), plane_l[...].reshape(256, 512)).astype(BF)
-    swap_d = remote(part_out, part_in, core_s.at[1], core_r.at[1], mate, c)
-    swap_d.start()
-    sent.append(swap_d.wait_send)
-    for m in range(COLS // 2):
-        cols = plane_r[:, :, :, m * L : (m + 1) * L].reshape(512, L)
-        split(nn(plane_d[...].reshape(256, 512), cols), out_p.at[1], m)
-    leg_send(4, out_p.at[1].reshape(CHIPS * COLS, T, L), in_h.at[1])
-    pltpu.make_async_copy(part_in, part_in, core_r.at[1]).wait()
-    for m in range(COLS // 2):
-        cols = plane_l[:, :, m * L : (m + 1) * L].reshape(256, L)
-        own = nn(grad_t[:, q].reshape(256, 256), cols)
-        split(own + part_in[:, m * L : (m + 1) * L].astype(F32), out_p.at[2], m)
-    leg_send(5, out_p.at[2].reshape(CHIPS * COLS, T, L), in_h.at[2])
 
     leg_wait(4, in_h.at[1])
     work_l[...] = in_h[1].astype(F32)
@@ -235,31 +273,24 @@
     w_send[:, 0] = grads[:, 0 : 3 * L].reshape(16, 8, 3 * L)
     w_send[:, 1] = grads[:, 3 * L : 6 * L].reshape(16, 8, 3 * L)
 
-    def near(j):
-        to = lax.rem(flat + j, 32)
-        return to // 2, lax.rem(to, 2), 2 * (lax.rem(to // 2, 2) * DEPTH + z) + lax.rem(to, 2), to // 4
-
-    def w1_copy(j):
-        block, core, row, col = near(j)
+    def plane_send(copy, n):
+        @pl.loop(1, 16, unroll=UNROLL)
+        def _(k):
+            base, col = place(16 - k)
+            row, block = 2 * (base + z), col * 2 + base // DEPTH
+            for core in (q, 1 - q):
+                copy(block, core, row + core, col).start()
+
+        copy(c * 2 + y, 1 - q, mate, c).start()
+        sent.append(pltpu.make_async_copy(w_recv.at[0:31], w_recv.at[0:31], wt_s.at[n]).wait)
+
+    def w1_copy(block, core, row, col):
         return remote(w_send.at[block, core], w_recv.at[flat], wt_s.at[0], wt_r.at[0], row, col)
 
-    def w2_copy(j):
-        row = 2 * (y * DEPTH + lax.rem(z + j, DEPTH)) + q
-        return remote(w_sum, w_all.at[z], wt_s.at[1], wt_r.at[1], row, c)
-
-    def w3_copy(j):
-        block, core, row, col = near(j)
+    def w3_copy(block, core, row, col):
         return remote(w_full, w_gather.at[flat], wt_s.at[2], wt_r.at[2], row, col)
 
-    def each(copy, count, n, whole):
-        @pl.loop(1, count)
-        def _(j):
-            copy(j).start()
-
-        rest = whole.at[0 : count - 1]
-        sent.append(pltpu.make_async_copy(rest, rest, wt_s.at[n]).wait)
-
-    each(w1_copy, 32, 0, w_recv)
+    plane_send(w1_copy, 0)
     pltpu.make_async_copy(w_send.at[c * 2 + y, q], w_recv.at[flat], wt_r.at[0]).start()
 
     for t in range(T):
@@ -268,40 +299,52 @@
         dpair_ref[t] = d[0 : L // 2]
         dpair_ref[t + T] = d[L // 2 : L]
 
+    store = pltpu.make_async_copy(dpair_ref, dpair_hbm, io_sem.at[4])
+    store.start()
     pltpu.make_async_copy(w_recv, w_recv, wt_r.at[0]).wait()
     w_sum[...] = jnp.sum(w_recv[...].astype(F32), axis=0).astype(BF)
-    each(w2_copy, DEPTH, 1, w_all)
+    for level in levels[:-1]:
+        remote(w_sum, w_all.at[z], wt_s.at[1], wt_r.at[1], 2 * (y * DEPTH + level) + q, c).start()
+    sent.append(pltpu.make_async_copy(w_all.at[1:DEPTH], w_all.at[1:DEPTH], wt_s.at[1]).wait)
     pltpu.make_async_copy(w_sum, w_all.at[z], wt_r.at[1]).start()
     pltpu.make_async_copy(w_all, w_all, wt_r.at[1]).wait()
     w_full[...] = jnp.sum(w_all[...].astype(F32), axis=0).astype(BF)
-    each(w3_copy, 32, 2, w_gather)
+    plane_send(w3_copy, 2)
     pltpu.make_async_copy(w_full, w_gather.at[flat], wt_r.at[2]).start()
     pltpu.make_async_copy(w_gather, w_gather, wt_r.at[2]).wait()
 
-    whole = w_gather[...].astype(F32).reshape(16, 2, 8, 3 * L)
-    first, second = whole[:, 0].reshape(L, 3 * L), whole[:, 1].reshape(L, 3 * L)
-    dwin_ref[:, 0 : 3 * L] = first
-    dwin_ref[:, 3 * L : 5 * L] = second[:, 0 : 2 * L]
-    dwout_ref[...] = second[:, 2 * L : 3 * L]
+    gather_ref[...] = w_gather[...]
+    store.wait()
 
     for wait in sent:
         wait()
+
+
+def finish_kernel(dpair_in, gather_ref, dpair_out, dwin_ref, dwout_ref):
+    dpair_out[...] = dpair_in[...]
+
+    @pl.when(pl.program_id(0) == 0)
+    def _():
+        whole = gather_ref[...].astype(F32).reshape(16, 2, 8, 3 * L)
+        first, second = whole[:, 0].reshape(L, 3 * L), whole[:, 1].reshape(L, 3 * L)
+        dwin_ref[:, 0 : 3 * L] = first
+        dwin_ref[:, 3 * L : 5 * L] = second[:, 0 : 2 * L]
+        dwout_ref[...] = second[:, 2 * L : 3 * L]
 
 
 def body(pair, pair_mask, in_gain, in_bias, w_in, out_gain, out_bias, w_out, cotangent):
     V = pltpu.VMEM
     tile = lambda dtype: V((T, L, L), dtype)
     D = pltpu.SemaphoreType.DMA
-    return pl.pallas_call(
+    vmem, hbm = pl.BlockSpec(memory_space=pltpu.VMEM), pl.BlockSpec(memory_space=pl.ANY)
+    d_pair, gathered = pl.pallas_call(
         kernel,
-        out_shape=(
-            jax.ShapeDtypeStruct(pair.shape, F32),
-            jax.ShapeDtypeStruct(w_in.shape, F32),
-            jax.ShapeDtypeStruct(w_out.shape, F32),
-        ),
-        in_specs=[pl.BlockSpec(memory_space=pltpu.VMEM)] * 9,
-        out_specs=[pl.BlockSpec(memory_space=pltpu.VMEM)] * 3,
+        out_shape=(jax.ShapeDtypeStruct(pair.shape, F32), jax.ShapeDtypeStruct((32, 8, 3 * L), BF)),
+        in_specs=[hbm, vmem, vmem, vmem, hbm, vmem, vmem, hbm, hbm],
+        out_specs=(hbm, vmem),
         scratch_shapes=[
+            V(pair.shape, F32), V(w_in.shape, BF), V(w_out.shape, BF), V(pair.shape, F32), V(pair.shape, F32), D((5,)),
+            pltpu.SemaphoreType.REGULAR,
             V((4, L, L), F32), V((5 * L, L), BF), V((L, L), BF), V((T, L), F32), tile(F32), V((T, L), F32), V((L, T * L), BF),
             tile(F32), tile(F32), tile(F32), tile(F32), tile(F32), V((L, T * L), BF), V((L, T, L), F32),
             V((L, T * L), BF), V((5 * L, T * L), BF), V((L, L), F32),
@@ -321,6 +364,19 @@
         pair, pair_mask, in_gain.reshape(1, L), in_bias.reshape(1, L), w_in,
         out_gain.reshape(1, L), out_bias.reshape(1, L), w_out, cotangent,
     )
+    block = pl.BlockSpec((4, 64, L), lambda n: (n, 0, 0))
+    whole = lambda shape: pl.BlockSpec(shape, lambda n: (0,) * len(shape))
+    return pl.pallas_call(
+        finish_kernel,
+        grid=(4,),
+        out_shape=(
+            jax.ShapeDtypeStruct(pair.shape, F32),
+            jax.ShapeDtypeStruct(w_in.shape, F32),
+            jax.ShapeDtypeStruct(w_out.shape, F32),
+        ),
+        in_specs=[block, whole((32, 8, 3 * L))],
+        out_specs=(block, whole(w_in.shape), whole(w_out.shape)),
+    )(d_pair, gathered)
 
 
 def solution(mesh):

time: 90 us -> 86.3 us (0.959)
  local copies, waits for them, and re-layouts: 3.43 us -> 0 us
    pallas_call x1, Pallas kernels: 85.8 us -> 82 us  [body(): pl.pallas_call(kernel, out_shape=(jax.ShapeDtypeStruct(pair.shape, F32),...]
    unnamed x7 -> x0, local copies, waits for them, and re-layouts: 3.43 us -> none
    pallas_call x0 -> x1, Pallas kernels: none -> 3.41 us  [body(): pl.pallas_call(finish_kernel, grid=(4,), out_shape=(jax.ShapeDtypeStruct(...]
where the time goes in v4:
time: 86.3 us; the launch traced here: 86.1 us
  Pallas kernels  85.4 us (99%)
    pallas_call x1, Pallas kernels, body(): pl.pallas_call(kernel, out_shape=(jax.ShapeDtypeStruct(pair.shape, F32),...  82 us
    pallas_call x1, Pallas kernels, body(): pl.pallas_call(finish_kernel, grid=(4,), out_shape=(jax.ShapeDtypeStruct(...  3.41 us

profile of v4, /device:TPU:1, one launch (start us, length us, event | category | flops | bytes accessed | tf_op | source)
XLA Modules:
  0.0 86.1 jit_solution(3018857264035997811)
XLA Ops:
  0.6 82.0 %shard_map.112 = (f32[16,64,128]{2,1,0:T(8,128)}, bf16[32,8,384]{2,1,0:T(8,128)(2,1)}) custom-call(f32[16,64,128]{2,1,0:T(8,128)} %pair_hbm.1, s32[16,64]{1,0:T(8,128)} %mask_ref.1, f32[1,128]{1,0:T(1,128)} %bitcast.4, f32[1,128]{1,0:T(1,128)} %bitcast.5, bf16[128,640]{1,0:T(8,128)(2,1)} %w_in_hbm.1, f32[1,128]{1,0:T(1,128)} %bitcast.6, f32[1,128]{1,0:T(1,128)} %bitcast.7, ...), custom_call_target="tpu_custom_call" | custom-call | tf_op jit(solution)/shard_map/pallas_call | solution.py:340
  82.7 3.4 %shard_map.113 = (f32[16,64,128]{2,1,0:T(8,128)}, f32[128,640]{1,0:T(8,128)}, f32[128,128]{1,0:T(8,128)}) custom-call(f32[16,64,128]{2,1,0:T(8,128)} %get-tuple-element.5.dpair_in, bf16[32,8,384]{2,1,0:T(8,128)(2,1)} %get-tuple-element.6.gather_ref), custom_call_target="tpu_custom_call" | custom-call | tf_op jit(solution)/shard_map/pallas_call | solution.py:369

commit v5 on v4

--- a/solution.py
+++ b/solution.py
@@ -71,7 +71,7 @@
     fa1, fa2, fb1, fb2, fgo, dmix, dxn, xn, dproj, dwout,
     out_h, in_h, out_p, in_p, plane_l, plane_r, plane_d, grad_t, work_r, work_l,
     part_out, part_in,
-    w_send, w_recv, w_sum, w_all, w_full, w_gather,
+    send_a, recv_a, send_b, recv_b, w_sum, w_all, w_full, w_gather,
     leg_s, leg_r, core_s, core_r, wt_s, wt_r,
 ):
     r, c = lax.axis_index("row"), lax.axis_index("col")
@@ -189,13 +189,14 @@
         hello(planes, 2 * (y * DEPTH + level) + q, c)
     hello(planes, mate, c)
     leg_send(0, out_h.at[0], in_p.at[0], near_chips)
+    for t in range(T):
+        side(t, 0, fa1, fa2, work_l)
+    out_h[1] = work_l[...].astype(BF)
+    leg_send(1, out_h.at[1], in_p.at[1], near_chips)
     pl.semaphore_wait(planes, DEPTH)
     leg_send(0, out_h.at[0], in_p.at[0], far_chips)
 
-    for t in range(T):
-        side(t, 0, fa1, fa2, work_l)
-    out_h[1] = work_l[...].astype(BF)
-    leg_send(1, out_h.at[1], in_p.at[1])
+    leg_send(1, out_h.at[1], in_p.at[1], far_chips)
 
     loads[3].wait()
     for t in range(T):
@@ -262,18 +263,7 @@
         d = work_l[:, t, :]
         dproj[0:L, t * L : (t + 1) * L] = (d * fa1[t]).astype(BF)
         dproj[L : 2 * L, t * L : (t + 1) * L] = (d * fa2[t]).astype(BF)
-    leg_wait(5, in_h.at[2])
-    work_r[...] = in_h[2].astype(F32)
-    for t in range(T):
-        d = work_r[:, t, :]
-        dproj[2 * L : 3 * L, t * L : (t + 1) * L] = (d * fb1[t]).astype(BF)
-        dproj[3 * L : 4 * L, t * L : (t + 1) * L] = (d * fb2[t]).astype(BF)
-
-    grads = jnp.concatenate([nt(zn[...], dproj[...]), dwout[...]], axis=1).astype(BF)
-    w_send[:, 0] = grads[:, 0 : 3 * L].reshape(16, 8, 3 * L)
-    w_send[:, 1] = grads[:, 3 * L : 6 * L].reshape(16, 8, 3 * L)
-
-    def plane_send(copy, n):
+    def plane_send(copy, n, whole):
         @pl.loop(1, 16, unroll=UNROLL)
         def _(k):
             base, col = place(16 - k)
@@ -282,16 +272,34 @@
                 copy(block, core, row + core, col).start()
 
         copy(c * 2 + y, 1 - q, mate, c).start()
-        sent.append(pltpu.make_async_copy(w_recv.at[0:31], w_recv.at[0:31], wt_s.at[n]).wait)
-
-    def w1_copy(block, core, row, col):
-        return remote(w_send.at[block, core], w_recv.at[flat], wt_s.at[0], wt_r.at[0], row, col)
+        sent.append(pltpu.make_async_copy(whole.at[0:31], whole.at[0:31], wt_s.at[n]).wait)
+
+    def scatter(n, grads, w_send, w_recv):
+        width = grads.shape[1] // 2
+        w_send[:, 0] = grads[:, 0:width].astype(BF).reshape(16, 8, width)
+        w_send[:, 1] = grads[:, width:].astype(BF).reshape(16, 8, width)
+
+        def copy(block, core, row, col):
+            return remote(w_send.at[block, core], w_recv.at[flat], wt_s.at[n], wt_r.at[n], row, col)
+
+        plane_send(copy, n, w_recv)
+        pltpu.make_async_copy(w_send.at[c * 2 + y, q], w_recv.at[flat], wt_r.at[n]).start()
 
     def w3_copy(block, core, row, col):
         return remote(w_full, w_gather.at[flat], wt_s.at[2], wt_r.at[2], row, col)
 
-    plane_send(w1_copy, 0)
-    pltpu.make_async_copy(w_send.at[c * 2 + y, q], w_recv.at[flat], wt_r.at[0]).start()
+    mine = nt(zn[...], dproj[0 : 2 * L, :])
+    gate = nt(zn[...], dproj[4 * L : 5 * L, :])
+    scatter(0, jnp.concatenate([mine, gate, dwout[...]], axis=1), send_a, recv_a)
+
+    leg_wait(5, in_h.at[2])
+    work_r[...] = in_h[2].astype(F32)
+    for t in range(T):
+        d = work_r[:, t, :]
+        dproj[2 * L : 3 * L, t * L : (t + 1) * L] = (d * fb1[t]).astype(BF)
+        dproj[3 * L : 4 * L, t * L : (t + 1) * L] = (d * fb2[t]).astype(BF)
+
+    scatter(3, nt(zn[...], dproj[2 * L : 4 * L, :]), send_b, recv_b)
 
     for t in range(T):
         dn = nn(w_in_ref[...], dproj[:, t * L : (t + 1) * L]) * gains[0]
@@ -301,15 +309,17 @@
 
     store = pltpu.make_async_copy(dpair_ref, dpair_hbm, io_sem.at[4])
     store.start()
-    pltpu.make_async_copy(w_recv, w_recv, wt_r.at[0]).wait()
-    w_sum[...] = jnp.sum(w_recv[...].astype(F32), axis=0).astype(BF)
+    pltpu.make_async_copy(recv_a, recv_a, wt_r.at[0]).wait()
+    pltpu.make_async_copy(recv_b, recv_b, wt_r.at[3]).wait()
+    w_sum[:, 0 : 2 * L] = jnp.sum(recv_a[...].astype(F32), axis=0).astype(BF)
+    w_sum[:, 2 * L :] = jnp.sum(recv_b[...].astype(F32), axis=0).astype(BF)
     for level in levels[:-1]:
         remote(w_sum, w_all.at[z], wt_s.at[1], wt_r.at[1], 2 * (y * DEPTH + level) + q, c).start()
     sent.append(pltpu.make_async_copy(w_all.at[1:DEPTH], w_all.at[1:DEPTH], wt_s.at[1]).wait)
     pltpu.make_async_copy(w_sum, w_all.at[z], wt_r.at[1]).start()
     pltpu.make_async_copy(w_all, w_all, wt_r.at[1]).wait()
     w_full[...] = jnp.sum(w_all[...].astype(F32), axis=0).astype(BF)
-    plane_send(w3_copy, 2)
+    plane_send(w3_copy, 2, w_gather)
     pltpu.make_async_copy(w_full, w_gather.at[flat], wt_r.at[2]).start()
     pltpu.make_async_copy(w_gather, w_gather, wt_r.at[2]).wait()
 
@@ -328,8 +338,9 @@
         whole = gather_ref[...].astype(F32).reshape(16, 2, 8, 3 * L)
         first, second = whole[:, 0].reshape(L, 3 * L), whole[:, 1].reshape(L, 3 * L)
         dwin_ref[:, 0 : 3 * L] = first
-        dwin_ref[:, 3 * L : 5 * L] = second[:, 0 : 2 * L]
-        dwout_ref[...] = second[:, 2 * L : 3 * L]
+        dwin_ref[:, 3 * L : 4 * L] = second[:, 2 * L : 3 * L]
+        dwin_ref[:, 4 * L : 5 * L] = second[:, 0:L]
+        dwout_ref[...] = second[:, L : 2 * L]
 
 
 def body(pair, pair_mask, in_gain, in_bias, w_in, out_gain, out_bias, w_out, cotangent):
@@ -353,9 +364,9 @@
             V((CHIPS, 16, 512), BF), V((CHIPS, 2, 16, 512), BF), V((CHIPS, 16, 512), BF), V((CHIPS, 2, 16, 256), BF),
             V((L, T, L), F32), V((L, T, L), F32),
             V((256, 512), BF), V((256, 512), BF),
-            V((16, 2, 8, 3 * L), BF), V((32, 8, 3 * L), BF), V((8, 3 * L), BF), V((DEPTH, 8, 3 * L), BF),
+            V((16, 2, 8, 2 * L), BF), V((32, 8, 2 * L), BF), V((16, 2, 8, L), BF), V((32, 8, L), BF), V((8, 3 * L), BF), V((DEPTH, 8, 3 * L), BF),
             V((8, 3 * L), BF), V((32, 8, 3 * L), BF),
-            D((6,)), D((6,)), D((2,)), D((2,)), D((3,)), D((3,)),
+            D((6,)), D((6,)), D((2,)), D((2,)), D((4,)), D((4,)),
         ],
         compiler_params=pltpu.CompilerParams(
             collective_id=0, has_side_effects=True, vmem_limit_bytes=60 * 1024 * 1024
@@ -364,11 +375,11 @@
         pair, pair_mask, in_gain.reshape(1, L), in_bias.reshape(1, L), w_in,
         out_gain.reshape(1, L), out_bias.reshape(1, L), w_out, cotangent,
     )
-    block = pl.BlockSpec((4, 64, L), lambda n: (n, 0, 0))
+    block = pl.BlockSpec((8, 64, L), lambda n: (n, 0, 0))
     whole = lambda shape: pl.BlockSpec(shape, lambda n: (0,) * len(shape))
     return pl.pallas_call(
         finish_kernel,
-        grid=(4,),
+        grid=(2,),
         out_shape=(
             jax.ShapeDtypeStruct(pair.shape, F32),
             jax.ShapeDtypeStruct(w_in.shape, F32),

time: 86.3 us -> 84.2 us (0.976)
  Pallas kernels: 85.4 us -> 83.4 us
    pallas_call x1, Pallas kernels: 3.41 us -> 1.99 us  [body(): pl.pallas_call(finish_kernel, grid=(2,), out_shape=(jax.ShapeDtypeStruct(...]
where the time goes in v5:
time: 84.2 us; the launch traced here: 84 us
  Pallas kernels  83.4 us (99%)
    pallas_call x1, Pallas kernels, body(): pl.pallas_call(kernel, out_shape=(jax.ShapeDtypeStruct(pair.shape, F32),...  81.4 us
    pallas_call x1, Pallas kernels, body(): pl.pallas_call(finish_kernel, grid=(2,), out_shape=(jax.ShapeDtypeStruct(...  1.99 us

profile of v5, /device:TPU:1, one launch (start us, length us, event | category | flops | bytes accessed | tf_op | source)
XLA Modules:
  0.0 84.0 jit_solution(10950057085068769237)
XLA Ops:
  0.6 81.4 %shard_map.112 = (f32[16,64,128]{2,1,0:T(8,128)}, bf16[32,8,384]{2,1,0:T(8,128)(2,1)}) custom-call(f32[16,64,128]{2,1,0:T(8,128)} %pair_hbm.1, s32[16,64]{1,0:T(8,128)} %mask_ref.1, f32[1,128]{1,0:T(1,128)} %bitcast.4, f32[1,128]{1,0:T(1,128)} %bitcast.5, bf16[128,640]{1,0:T(8,128)(2,1)} %w_in_hbm.1, f32[1,128]{1,0:T(1,128)} %bitcast.6, f32[1,128]{1,0:T(1,128)} %bitcast.7, ...), custom_call_target="tpu_custom_call" | custom-call | tf_op jit(solution)/shard_map/pallas_call | solution.py:351
  82.0 2.0 %shard_map.113 = (f32[16,64,128]{2,1,0:T(8,128)}, f32[128,640]{1,0:T(8,128)}, f32[128,128]{1,0:T(8,128)}) custom-call(f32[16,64,128]{2,1,0:T(8,128)} %get-tuple-element.5.dpair_in, bf16[32,8,384]{2,1,0:T(8,128)(2,1)} %get-tuple-element.6.gather_ref), custom_call_target="tpu_custom_call" | custom-call | tf_op jit(solution)/shard_map/pallas_call | solution.py:380

commit v6 on v5

--- a/solution.py
+++ b/solution.py
@@ -64,9 +64,10 @@
 
 
 def kernel(
-    pair_hbm, mask_ref, in_gain_ref, in_bias_ref, w_in_hbm, out_gain_ref, out_bias_ref, w_out_hbm, cot_hbm,
+    pair_hbm, mask_hbm, in_gain_hbm, in_bias_hbm, w_in_hbm, out_gain_hbm, out_bias_hbm, w_out_hbm, cot_hbm,
     dpair_hbm, gather_ref,
-    pair_ref, w_in_ref, w_out_ref, cot_ref, dpair_ref, io_sem, planes,
+    pair_ref, mask_ref, in_gain_ref, in_bias_ref, w_in_ref, out_gain_ref, out_bias_ref, w_out_ref, cot_ref,
+    dpair_ref, io_sem, planes,
     gains, w_in_t, w_out_t, mask_rows, in_normed, in_inv, zn,
     fa1, fa2, fb1, fb2, fgo, dmix, dxn, xn, dproj, dwout,
     out_h, in_h, out_p, in_p, plane_l, plane_r, plane_d, grad_t, work_r, work_l,
@@ -85,7 +86,11 @@
     loads = [
         pltpu.make_async_copy(src, dst, io_sem.at[n])
         for n, (src, dst) in enumerate(
-            ((pair_hbm, pair_ref), (w_in_hbm, w_in_ref), (w_out_hbm, w_out_ref), (cot_hbm, cot_ref))
+            (
+                (pair_hbm, pair_ref), (mask_hbm, mask_ref), (in_gain_hbm, in_gain_ref), (in_bias_hbm, in_bias_ref),
+                (w_in_hbm, w_in_ref), (out_gain_hbm, out_gain_ref), (out_bias_hbm, out_bias_ref), (w_out_hbm, w_out_ref),
+                (cot_hbm, cot_ref),
+            )
         )
     ]
     for load in loads:
@@ -155,12 +160,12 @@
     def blocks(ref):
         return ref[...].reshape(CHIPS, COLS, T, L)
 
+    for load in loads[:8]:
+        load.wait()
     gains[0] = spread(in_gain_ref)
     gains[1] = spread(in_bias_ref)
     gains[2] = spread(out_gain_ref)
     gains[3] = spread(out_bias_ref)
-    for load in loads[:3]:
-        load.wait()
     w_in_t[...] = w_in_ref[...].astype(F32).T.astype(BF)
     w_out_t[...] = w_out_ref[...].astype(F32).T.astype(BF)
     mask_f = mask_ref[...].astype(F32)
@@ -198,7 +203,7 @@
 
     leg_send(1, out_h.at[1], in_p.at[1], far_chips)
 
-    loads[3].wait()
+    loads[8].wait()
     for t in range(T):
         gate = jax.nn.sigmoid(nn(w_in_t[4 * L : 5 * L, :], zn[:, t * L : (t + 1) * L]))
         cot = jnp.concatenate([cot_ref[t], cot_ref[t + T]], axis=0).T
@@ -307,7 +312,7 @@
         dpair_ref[t] = d[0 : L // 2]
         dpair_ref[t + T] = d[L // 2 : L]
 
-    store = pltpu.make_async_copy(dpair_ref, dpair_hbm, io_sem.at[4])
+    store = pltpu.make_async_copy(dpair_ref, dpair_hbm, io_sem.at[9])
     store.start()
     pltpu.make_async_copy(recv_a, recv_a, wt_r.at[0]).wait()
     pltpu.make_async_copy(recv_b, recv_b, wt_r.at[3]).wait()
@@ -351,10 +356,11 @@
     d_pair, gathered = pl.pallas_call(
         kernel,
         out_shape=(jax.ShapeDtypeStruct(pair.shape, F32), jax.ShapeDtypeStruct((32, 8, 3 * L), BF)),
-        in_specs=[hbm, vmem, vmem, vmem, hbm, vmem, vmem, hbm, hbm],
+        in_specs=[hbm] * 9,
         out_specs=(hbm, vmem),
         scratch_shapes=[
-            V(pair.shape, F32), V(w_in.shape, BF), V(w_out.shape, BF), V(pair.shape, F32), V(pair.shape, F32), D((5,)),
+            V(pair.shape, F32), V(pair_mask.shape, jnp.int32), V((1, L), F32), V((1, L), F32), V(w_in.shape, BF),
+            V((1, L), F32), V((1, L), F32), V(w_out.shape, BF), V(pair.shape, F32), V(pair.shape, F32), D((10,)),
             pltpu.SemaphoreType.REGULAR,
             V((4, L, L), F32), V((5 * L, L), BF), V((L, L), BF), V((T, L), F32), tile(F32), V((T, L), F32), V((L, T * L), BF),
             tile(F32), tile(F32), tile(F32), tile(F32), tile(F32), V((L, T * L), BF), V((L, T, L), F32),

time: 84.2 us -> 83.3 us (0.989)
  Pallas kernels: 83.4 us -> 82.5 us
    pallas_call x1, Pallas kernels: 81.4 us -> 80.5 us  [body(): pl.pallas_call(kernel, out_shape=(jax.ShapeDtypeStruct(pair.shape, F32),...]
where the time goes in v6:
time: 83.3 us; the launch traced here: 83.1 us
  Pallas kernels  82.5 us (99%)
    pallas_call x1, Pallas kernels, body(): pl.pallas_call(kernel, out_shape=(jax.ShapeDtypeStruct(pair.shape, F32),...  80.5 us
    pallas_call x1, Pallas kernels, body(): pl.pallas_call(finish_kernel, grid=(2,), out_shape=(jax.ShapeDtypeStruct(...  1.99 us

profile of v6, /device:TPU:1, one launch (start us, length us, event | category | flops | bytes accessed | tf_op | source)
XLA Modules:
  0.0 83.1 jit_solution(7113487783159302401)
XLA Ops:
  0.6 80.5 %shard_map.112 = (f32[16,64,128]{2,1,0:T(8,128)}, bf16[32,8,384]{2,1,0:T(8,128)(2,1)}) custom-call(f32[16,64,128]{2,1,0:T(8,128)} %pair_hbm.1, s32[16,64]{1,0:T(8,128)} %mask_hbm.1, f32[1,128]{1,0:T(1,128)} %bitcast.4, f32[1,128]{1,0:T(1,128)} %bitcast.5, bf16[128,640]{1,0:T(8,128)(2,1)} %w_in_hbm.1, f32[1,128]{1,0:T(1,128)} %bitcast.6, f32[1,128]{1,0:T(1,128)} %bitcast.7, ...), custom_call_target="tpu_custom_call" | custom-call | tf_op jit(solution)/shard_map/pallas_call | solution.py:356
  81.2 2.0 %shard_map.113 = (f32[16,64,128]{2,1,0:T(8,128)}, f32[128,640]{1,0:T(8,128)}, f32[128,128]{1,0:T(8,128)}) custom-call(f32[16,64,128]{2,1,0:T(8,128)} %get-tuple-element.5.dpair_in, bf16[32,8,384]{2,1,0:T(8,128)(2,1)} %get-tuple-element.6.gather_ref), custom_call_target="tpu_custom_call" | custom-call | tf_op jit(solution)/shard_map/pallas_call | solution.py:386
